TPU v7x, 32 devices: a whole 2x2x4 slice. The times are simulated.
32 devices in a mesh: grp: 4 (over y, x), dev: 8 (over z, core).
Axes of the slice: x: 2, y: 2, z: 4, core: 2. Of those that a mesh axis runs over, the one named last changes fastest.
Arguments:
- queries: bfloat16 [4096, 4096], P('dev', 'grp'), may hold values from -120 to 120
- keys: bfloat16 [4096, 512], P('dev', 'grp'), may hold values from -4.5 to 4.5
- values: bfloat16 [4096, 512], P('dev', 'grp'), may hold values from -6 to 6
- doc_ids: int32 [4096], replicated, may hold values from 0 to 15, never falling along the last dimension, each value on 1 to 2560 neighbouring positions
- out_weight: bfloat16 [4096, 2048], P('grp'), may hold values from -0.5 to 0.5
- norm_gain: float32 [2048], replicated, may hold values from 0.1 to 1.9
- expert_ids: int32 [8, 512, 8], P('dev', 'grp'), may hold values from 0 to 31, all different within a row; in each aligned block of 128 rows (0 to 127, 128 to 255, ..., all dimensions but the last counted through in order) at most 48 rows name the same one
- gate_values: float32 [8, 512, 8], P('dev', 'grp'), may hold values from 0.05 to 0.5
- expert_gate: bfloat16 [32, 2048, 768], P(('grp', 'dev')), may hold values from -0.125 to 0.125
- expert_up: bfloat16 [32, 2048, 768], P(('grp', 'dev')), may hold values from -0.125 to 0.125
- expert_down: bfloat16 [32, 768, 2048], P(('grp', 'dev')), may hold values from -0.21875 to 0.21875
Outputs:
- final: bfloat16 [8, 512, 2048], P('dev', 'grp')
Inputs may be any that keep to these rules, and one draw needn't show every extreme that they name: doc_ids never fall along the tokens; every document has 1 to 2560 tokens and one has exactly 2560. `expert_ids`: each token names 8 different experts; among the 128 tokens of one device no expert is named by more than 48 tokens, and some expert reaches 48.
All inputs are finite; a program needn't handle non-finite values.
Results may differ from a plain program's by a relative error of at most 0.017.
Values may be sent and summed in bfloat16 or wider, within the bound.
No kernel may reach another device: no remote copies, remote signals or barrier semaphores. Data moves between devices by JAX's collectives and lax.ppermute only.
A program may use at most 128 MiB of HBM per device.

v0:
```python
import math

import jax
import jax.numpy as jnp
from jax import lax
from jax.sharding import PartitionSpec as P

HEAD_SIZE = 128


def shifted(value, axis, steps):
    count = lax.axis_size(axis)
    leading, last = (max(0, -steps), min(count, count - steps))
    return lax.ppermute(value, axis, [(source, source + steps) for source in range(leading, last)])


def shards(
    queries,
    keys,
    values,
    doc_ids,
    out_weight,
    norm_gain,
    expert_ids,
    gate_values,
    expert_gate,
    expert_up,
    expert_down,
):
    own_rows = queries.shape[0]
    key_heads = keys.shape[1] // HEAD_SIZE
    query_heads = queries.shape[1] // HEAD_SIZE
    shared_heads = query_heads // key_heads
    scaling = 1.0 / math.sqrt(HEAD_SIZE)
    row_offset = lax.axis_index("dev") * own_rows
    query_pos = row_offset + jnp.arange(own_rows, dtype=jnp.int32)
    query_doc = lax.dynamic_slice_in_dim(doc_ids, row_offset, own_rows, 0)
    query_blocks = queries.reshape(own_rows, key_heads, shared_heads, HEAD_SIZE)

    def absorb(folded, shard_piece, anchor):
        key_piece, value_piece = shard_piece
        length = key_piece.shape[0]
        block_row_count = math.gcd(length, 512)
        block_count = length // block_row_count

        def one_step(block_index, running):
            block_low = block_index * block_row_count
            key_block = key_piece.reshape(block_row_count, key_heads, HEAD_SIZE)
            value_block = value_piece.reshape(block_row_count, key_heads, HEAD_SIZE)
            key_pos = anchor + block_low + jnp.arange(block_row_count, dtype=jnp.int32)
            key_doc = lax.dynamic_slice_in_dim(doc_ids, anchor + block_low, block_row_count, 0)
            allowed = (
                (query_doc[:, None] == key_doc[None, :])
                & (key_pos[None, :] <= query_pos[:, None])
                & (key_pos[None, :] >= 0)
            )

            def update(current):
                maxima, totals, accums = current
                scores = (
                    jnp.einsum(
                        "qngd,knd->ngqk",
                        query_blocks,
                        key_block,
                        preferred_element_type=jnp.float32,
                    )
                    * scaling
                )
                scores = jnp.where(allowed, scores, -jnp.inf)
                new_max = jnp.maximum(maxima, jnp.max(scores, axis=-1))
                weights = jnp.where(allowed, jnp.exp(scores - new_max[..., None]), 0.0)
                factor = jnp.exp(maxima - new_max)
                totals = totals * factor + jnp.sum(weights, axis=-1)
                added = jnp.einsum(
                    "ngqk,knd->ngqd",
                    weights.astype(jnp.bfloat16),
                    value_block,
                    preferred_element_type=jnp.float32,
                )
                accums = accums * factor[..., None] + added
                return (new_max, totals, accums)

            return lax.cond(jnp.any(allowed), update, lambda current: current, running)

        return lax.fori_loop(0, block_count, one_step, folded)

    start_max = jnp.full((key_heads, shared_heads, own_rows), -1e30, jnp.float32)
    start_total = jnp.zeros((key_heads, shared_heads, own_rows), jnp.float32)
    start_accum = jnp.zeros((key_heads, shared_heads, own_rows, HEAD_SIZE), jnp.float32)
    grp_size = lax.axis_size("grp")
    dev_size = lax.axis_size("dev")
    doc_reach = dev_size * own_rows // 2 + own_rows
    shard_reach = min(dev_size - 1, (doc_reach + own_rows - 1) // own_rows)
    folded = absorb((start_max, start_total, start_accum), (keys, values), row_offset)
    for distance in range(1, shard_reach + 1):
        earlier = shifted((keys, values), "dev", distance)
        folded = absorb(folded, earlier, row_offset - distance * own_rows)
    maxima, totals, accums = folded
    attended = (
        (accums / totals[..., None])
        .transpose(2, 0, 1, 3)
        .reshape(own_rows, query_heads * HEAD_SIZE)
        .astype(jnp.bfloat16)
    )
    dev_rows = own_rows // grp_size
    model_width = out_weight.shape[1]
    projected = lax.psum_scatter(
        jnp.dot(attended, out_weight, preferred_element_type=jnp.float32).astype(jnp.bfloat16),
        "grp",
        scatter_dimension=0,
        tiled=True,
    ).astype(jnp.float32)
    normed = (
        projected
        * lax.rsqrt(jnp.mean(projected * projected, axis=-1, keepdims=True) + 1e-06)
        * norm_gain
    ).astype(jnp.bfloat16)
    routed_ids = expert_ids[0]
    gate_rows = gate_values[0]
    top_count = routed_ids.shape[1]
    expert_count = grp_size * dev_size
    capacity = max(2, 3 * dev_rows * top_count // (2 * expert_count))
    flat_ids = routed_ids.reshape(-1)
    onehot = (flat_ids[:, None] == jnp.arange(expert_count, dtype=jnp.int32)[None, :]).astype(
        jnp.int32
    )
    slot_rank = jnp.sum((jnp.cumsum(onehot, axis=0) - onehot) * onehot, axis=1)
    target = flat_ids * capacity + slot_rank
    placer = target[None, :] == jnp.arange(expert_count * capacity, dtype=jnp.int32)[:, None]
    placer = jnp.any(placer.reshape(expert_count * capacity, dev_rows, top_count), axis=2).astype(
        jnp.bfloat16
    )
    outgoing = jnp.dot(placer, normed, preferred_element_type=jnp.float32).astype(jnp.bfloat16)
    outgoing = outgoing.reshape(expert_count, capacity, model_width)
    arrived = lax.all_to_all(outgoing, ("grp", "dev"), split_axis=0, concat_axis=0, tiled=True)
    layout = arrived.shape
    stacked = arrived.reshape(-1, layout[-1])
    gate_act = jnp.dot(stacked, expert_gate[0], preferred_element_type=jnp.float32)
    up_act = jnp.dot(stacked, expert_up[0], preferred_element_type=jnp.float32)
    hidden = (jax.nn.silu(gate_act) * up_act).astype(jnp.bfloat16)
    produced = (
        jnp.dot(hidden, expert_down[0], preferred_element_type=jnp.float32)
        .astype(jnp.bfloat16)
        .reshape(layout)
    )
    returned = lax.all_to_all(produced, ("grp", "dev"), split_axis=0, concat_axis=0, tiled=True)
    returned = returned.reshape(expert_count * capacity, model_width)
    picked = returned[target].reshape(dev_rows, top_count, model_width).astype(jnp.float32)
    mixed = jnp.sum(picked * gate_rows[..., None], axis=1)
    final = (projected + mixed).astype(jnp.bfloat16)
    return final[None]


def solution(mesh):
    return jax.shard_map(
        shards,
        mesh=mesh,
        in_specs=(
            P("dev", "grp"),
            P("dev", "grp"),
            P("dev", "grp"),
            P(),
            P("grp", None),
            P(),
            P("dev", "grp", None),
            P("dev", "grp", None),
            P(("grp", "dev"), None, None),
            P(("grp", "dev"), None, None),
            P(("grp", "dev"), None, None),
        ),
        out_specs=P("dev", "grp", None),
        check_vma=False,
    )
```

profile of v0, /device:TPU:0, one launch (start us, length us, event | category | flops | bytes accessed | tf_op | source)
XLA Modules:
  0.0 488.5 jit_solution(7111138344178732880)
XLA Ops:
  6.5 2.6 collective-permute-start
  9.2 4.5 collective-permute-start.2
  13.7 4.0 collective-permute-start.1
  17.6 3.5 collective-permute-start.3
  25.6 2.5 collective-permute-start.5
  28.1 1.9 collective-permute-start.6
  30.0 1.9 collective-permute-start.7
  32.0 2.0 collective-permute-start.8
  34.0 1.9 collective-permute-start.9
  35.9 5.6 %and_and_fusion = (pred[512,512]{0,1:T(8,128)(4,1)}, pred[]{:T(512)}, pred[]{:T(512)}, pred[512,512]{0,1:T(8,128)(4,1)}, pred[]{:T(512)}, /*index=5*/pred[512,51...) fusion(s32[512]{0:T(512)S(1)} %get-tuple-element.578, ...), kind=kLoop, calls=%fused_computation.142 | loop fusion | flops 7864314 | bytes 1600518 | tf_op jit(solution)/shard_map/while/body/eval_jaxpr/and | solution.py:53
  45.3 2.3 copy.46
  49.1 9.4 %conditional.6 = ((f32[1,8,512]{2,1,0:T(8,128)S(1)}, f32[1,8,512]{2,1,0:T(8,128)S(1)}, f32[1,8,512,128]{3,2,1,0:T(8,128)})) conditional(s32[]{:T(128)} %convert_element_type.92, (f32[1,8,512]{2,1,0:T(8,128)S(1)}, f32[1,8,512]{2,1,0:T(8,128)S(1)}, f32[1,8,512,128]{3,2,1,0:T(8,128)}) %tuple.60, (pred[512,512]{0,1:T(8,128)(4,1)}, ...), branch_computations={%region_6.7_spmd, %region_7.10_spmd} | conditional | flops 1102065664 | bytes 50069648 | solution.py:83
  49.1 2.9 fusion
  52.0 2.0 fusion.2
  54.1 3.1 bitcast_add_fusion
  58.7 7.2 %conditional.10 = ((f32[1,8,512]{2,1,0:T(8,128)S(1)}, f32[1,8,512]{2,1,0:T(8,128)S(1)}, f32[1,8,512,128]{3,2,1,0:T(8,128)})) conditional(s32[]{:T(128)} %convert_element_type.88, (f32[1,8,512]{2,1,0:T(8,128)S(1)}, f32[1,8,512]{2,1,0:T(8,128)S(1)}, f32[1,8,512,128]{3,2,1,0:T(8,128)}) %get-tuple-element.623, (pred[512,512]{0,1:T(8,128)(4,1)}, ...), branch_computations={%region_22.0_spmd, %region_23.26_spmd} | conditional | flops 1102065664 | bytes 49545332 | solution.py:83
  66.0 6.1 %conditional.11 = (f32[1,8,512]{2,1,0:T(8,128)S(1)}, f32[1,8,512,128]{2,3,1,0:T(8,128)}) conditional(s32[]{:T(128)} %convert_element_type.87, (f32[1,8,512]{2,1,0:T(8,128)S(1)}, f32[1,8,512,128]{3,2,1,0:T(8,128)}) %tuple.66, (pred[512,512]{0,1:T(8,128)(4,1)S(1)}, bf16[512,1,8,128]{0,3,2,1:T(8,128)(2,1)}, bf16[512,128]{1,0:T(8,128)(2,1)}, ...), branch_computations={%region_26.27_spmd, %region_27.30_spmd} | conditional | flops 1102069760 | bytes 44269612 | solution.py:83
  66.0 2.9 copy.67
  74.0 6.0 %convolution_convert_fusion.2 = bf16[512,2048]{1,0:T(8,128)(2,1)} fusion(bf16[512,1024]{0,1:T(8,128)(2,1)S(1)} %bitcast.363, bf16[1024,2048]{1,0:T(8,128)(2,1)} %param.27), kind=kOutput, calls=%fused_computation.133 | convolution fusion | flops 2148532224 | bytes 7340032 | tf_op jit(solution)/shard_map/dot_general | solution.py:108
  80.3 9.0 %reduce-window.6 = s32[32,8,128]{2,1,0:T(8,128)S(1)} reduce-window(s32[32,8,128]{2,1,0:T(8,128)S(1)} %fusion.120, s32[]{:T(128)} %constant.119.clone.1), window={size=1x1x128 pad=0_0x0_0x127_0}, to_apply=%region_31.32 | reduce-window | flops 4161536 | bytes 262148 | tf_op jit(solution)/shard_map/reduce-window
  90.0 5.6 %fusion.104 = pred[1536,128]{1,0:T(8,128)(4,1)S(1)} fusion(s32[128,8]{0,1:T(8,128)S(1)} %copy.59), kind=kLoop, calls=%fused_computation.127 | loop fusion | flops 2949120 | bytes 200704 | tf_op jit(solution)/shard_map/reduce_or | solution.py:130
  95.6 54.5 %reduce-scatter.2.cloned.1.call-done = bf16[128,2048]{1,0:T(8,128)(2,1)} async-done(((bf16[512,2048]{1,0:T(8,128)(2,1)}), bf16[128,2048]{1,0:T(8,128)(2,1)}) %reduce-scatter.2.cloned.1.call-update) | async-done | bytes 524304 | tf_op jit(solution)/shard_map/reduce_scatter | solution.py:107
  151.3 2.9 convolution_convert_fusion.1
  154.3 144.5 %all_to_all.10 = bf16[32,48,2048]{2,1,0:T(8,128)(2,1)S(1)} all-to-all(bf16[32,48,2048]{2,1,0:T(8,128)(2,1)S(1)} %bitcast.358), channel_id=1, replica_groups=mesh['grp'=4,'dev'=8] {'grp','dev'}, dimensions={0} | all-to-all | bytes 12582912 | tf_op jit(solution)/shard_map/all_to_all | solution.py:135
  298.8 5.2 %fusion.107 = f32[1536,768]{1,0:T(8,128)S(1)} fusion(bf16[1536,2048]{1,0:T(8,128)(2,1)S(1)} %bitcast.360, bf16[1,2048,768]{2,1,0:T(8,128)(2,1)S(1)} %copy-done.23), kind=kOutput, calls=%fused_computation.131 | convolution fusion | flops 4831838208 | bytes 14155776 | tf_op jit(solution)/shard_map/dot_general | solution.py:138
  304.0 5.6 %multiply_convert_fusion = bf16[1536,768]{1,0:T(8,128)(2,1)S(1)} fusion(f32[1536,768]{1,0:T(8,128)S(1)} %fusion.107, bf16[1536,2048]{1,0:T(8,128)(2,1)S(1)} %bitcast.361, bf16[1,2048,768]{2,1,0:T(8,128)(2,1)S(1)} %copy-done.24), kind=kOutput, calls=%fused_computation.128 | convolution fusion | flops 4838916096 | bytes 16515072 | tf_op jit(solution)/shard_map/dot_general | solution.py:139
  309.6 7.0 %convolution_convert_fusion = bf16[1536,2048]{1,0:T(8,128)(2,1)} fusion(bf16[1536,768]{1,0:T(8,128)(2,1)S(1)} %multiply_convert_fusion, bf16[1,768,2048]{2,1,0:T(8,128)(2,1)S(1)} %copy-done), kind=kOutput, calls=%fused_computation.124 | convolution fusion | flops 4834983936 | bytes 11796480 | tf_op jit(solution)/shard_map/dot_general | solution.py:142
  316.7 4.0 all-to-all-start.1
  320.9 139.7 %all-to-all-done.1 = bf16[32,48,2048]{2,1,0:T(8,128)(2,1)} async-done(((bf16[32,48,2048]{2,1,0:T(8,128)(2,1)}), bf16[32,48,2048]{2,1,0:T(8,128)(2,1)}, u32[]{:S(2)}, u32[]{:S(2)}) %all-to-all-start.1) | async-done | bytes 6291488 | tf_op jit(solution)/shard_map/all_to_all | solution.py:146
  460.6 12.4 %gather_fusion = bf16[1024,2048]{1,0:T(8,128)(2,1)} fusion(bf16[1536,2048]{1,0:T(8,128)(2,1)} %bitcast.95, s32[1024]{0:T(1024)S(1)} %broadcast_clamp_fusion), kind=kCustom, calls=%fused_computation | custom fusion | bytes 8392704 | tf_op jit(solution)/shard_map/gather | solution.py:148
  473.0 6.5 %fusion.103 = f32[128,2048]{1,0:T(8,128)S(1)} fusion(bf16[1024,2048]{1,0:T(8,128)(2,1)} %gather_fusion, f32[128,8]{1,0:T(8,128)S(1)} %copy.60), kind=kLoop, calls=%fused_computation.123 | loop fusion | flops 6029312 | bytes 5246976 | tf_op jit(solution)/shard_map/reduce_sum | solution.py:149
  479.5 2.0 fusion.113
  (77 shorter events, 11.7 us)
Async XLA Ops:
  6.5 303.1 %copy-start = (bf16[1,768,2048]{2,1,0:T(8,128)(2,1)S(1)}, bf16[1,768,2048]{2,1,0:T(8,128)(2,1)}, u32[]{:S(2)}) copy-start(bf16[1,768,2048]{2,1,0:T(8,128)(2,1)} %param.33) | copy-start | bytes 9437188
  6.5 143.6 %reduce-scatter.2.cloned.1.call-start = ((), (), s32[]{:S(2)}) async-start(), calls=%async_computation.3 | async-start | bytes 2621440 | tf_op jit(solution)/shard_map/reduce_scatter | solution.py:107
  6.5 19.1 %collective-permute-start = (bf16[512,128]{1,0:T(8,128)(2,1)}, bf16[512,128]{1,0:T(8,128)(2,1)S(1)}, u32[]{:S(2)}, u32[]{:S(2)}) collective-permute-start(bf16[512,128]{1,0:T(8,128)(2,1)} %param.24), channel_id=1, source_target_pairs={{0,1},{1,2},{2,3},{3,4},{4,5},{5,6},{6,7},{8,9},{9,10},{10,11},{11... | collective-permute-start | bytes 393224 | tf_op jit(solution)/shard_map/ppermute | solution.py:14
  9.2 20.9 %collective-permute-start.2 = (bf16[512,128]{1,0:T(8,128)(2,1)}, bf16[512,128]{1,0:T(8,128)(2,1)S(1)}, u32[]{:S(2)}, u32[]{:S(2)}) collective-permute-start(bf16[512,128]{1,0:T(8,128)(2,1)} %param.24), channel_id=1, source_target_pairs={{0,2},{1,3},{2,4},{3,5},{4,6},{5,7},{8,10},{9,11},{10,12},{11,13},... | collective-permute-start | bytes 393224 | tf_op jit(solution)/shard_map/ppermute | solution.py:14
  13.7 14.4 %collective-permute-start.1 = (bf16[512,128]{1,0:T(8,128)(2,1)}, bf16[512,128]{1,0:T(8,128)(2,1)}, u32[]{:S(2)}, u32[]{:S(2)}) collective-permute-start(bf16[512,128]{1,0:T(8,128)(2,1)} %param.25), channel_id=1, source_target_pairs={{0,1},{1,2},{2,3},{3,4},{4,5},{5,6},{6,7},{8,9},{9,10},{10,11},{11... | collective-permute-start | bytes 393224 | tf_op jit(solution)/shard_map/ppermute | solution.py:14
  17.6 14.4 %collective-permute-start.3 = (bf16[512,128]{1,0:T(8,128)(2,1)}, bf16[512,128]{1,0:T(8,128)(2,1)}, u32[]{:S(2)}, u32[]{:S(2)}) collective-permute-start(bf16[512,128]{1,0:T(8,128)(2,1)} %param.25), channel_id=1, source_target_pairs={{0,2},{1,3},{2,4},{3,5},{4,6},{5,7},{8,10},{9,11},{10,12},{11,13},... | collective-permute-start | bytes 393224 | tf_op jit(solution)/shard_map/ppermute | solution.py:14
  21.1 12.8 %collective-permute-start.4 = (bf16[512,128]{1,0:T(8,128)(2,1)}, bf16[512,128]{1,0:T(8,128)(2,1)S(1)}, u32[]{:S(2)}, u32[]{:S(2)}) collective-permute-start(bf16[512,128]{1,0:T(8,128)(2,1)} %param.24), channel_id=1, source_target_pairs={{0,3},{1,4},{2,5},{3,6},{4,7},{8,11},{9,12},{10,13},{11,14},{12,15... | collective-permute-start | bytes 393224 | tf_op jit(solution)/shard_map/ppermute | solution.py:14
  25.6 10.3 %copy-start.19 = (bf16[512,128]{1,0:T(8,128)(2,1)}, bf16[512,128]{1,0:T(8,128)(2,1)S(1)}, u32[]{:S(2)}) copy-start(bf16[512,128]{1,0:T(8,128)(2,1)S(1)} %collective-permute-done) | copy-start | bytes 393220
  25.6 33.0 %collective-permute-start.5 = (bf16[512,128]{1,0:T(8,128)(2,1)}, bf16[512,128]{1,0:T(8,128)(2,1)}, u32[]{:S(2)}, u32[]{:S(2)}) collective-permute-start(bf16[512,128]{1,0:T(8,128)(2,1)} %param.25), channel_id=1, source_target_pairs={{0,3},{1,4},{2,5},{3,6},{4,7},{8,11},{9,12},{10,13},{11,14},{12,15... | collective-permute-start | bytes 393224 | tf_op jit(solution)/shard_map/ppermute | solution.py:14
  28.1 30.6 %collective-permute-start.6 = (bf16[512,128]{1,0:T(8,128)(2,1)}, bf16[512,128]{1,0:T(8,128)(2,1)}, u32[]{:S(2)}, u32[]{:S(2)}) collective-permute-start(bf16[512,128]{1,0:T(8,128)(2,1)} %param.24), channel_id=1, source_target_pairs={{0,4},{1,5},{2,6},{3,7},{8,12},{9,13},{10,14},{11,15},{16,20},{17,... | collective-permute-start | bytes 393224 | tf_op jit(solution)/shard_map/ppermute | solution.py:14
  30.0 5.9 %copy-start.18 = (bf16[512,128]{1,0:T(8,128)(2,1)}, bf16[512,128]{1,0:T(8,128)(2,1)S(1)}, u32[]{:S(2)}) copy-start(bf16[512,128]{1,0:T(8,128)(2,1)S(1)} %collective-permute-done.2) | copy-start | bytes 393220
  30.0 28.7 %collective-permute-start.7 = (bf16[512,128]{1,0:T(8,128)(2,1)}, bf16[512,128]{1,0:T(8,128)(2,1)}, u32[]{:S(2)}, u32[]{:S(2)}) collective-permute-start(bf16[512,128]{1,0:T(8,128)(2,1)} %param.25), channel_id=1, source_target_pairs={{0,4},{1,5},{2,6},{3,7},{8,12},{9,13},{10,14},{11,15},{16,20},{17,... | collective-permute-start | bytes 393224 | tf_op jit(solution)/shard_map/ppermute | solution.py:14
  32.0 34.0 %collective-permute-start.8 = (bf16[512,128]{1,0:T(8,128)(2,1)}, bf16[512,128]{1,0:T(8,128)(2,1)}, u32[]{:S(2)}, u32[]{:S(2)}) collective-permute-start(bf16[512,128]{1,0:T(8,128)(2,1)} %param.24), channel_id=1, source_target_pairs={{0,5},{1,6},{2,7},{8,13},{9,14},{10,15},{16,21},{17,22},{18,23},{2... | collective-permute-start | bytes 393224 | tf_op jit(solution)/shard_map/ppermute | solution.py:14
  34.0 2.0 copy-start.17
  34.0 32.0 %collective-permute-start.9 = (bf16[512,128]{1,0:T(8,128)(2,1)}, bf16[512,128]{1,0:T(8,128)(2,1)}, u32[]{:S(2)}, u32[]{:S(2)}) collective-permute-start(bf16[512,128]{1,0:T(8,128)(2,1)} %param.25), channel_id=1, source_target_pairs={{0,5},{1,6},{2,7},{8,13},{9,14},{10,15},{16,21},{17,22},{18,23},{2... | collective-permute-start | bytes 393224 | tf_op jit(solution)/shard_map/ppermute | solution.py:14
  49.1 2.9 copy-start.16
  49.1 5.0 %copy-start.1 = (f32[1,8,512,128]{3,2,1,0:T(8,128)S(1)}, f32[1,8,512,128]{3,2,1,0:T(8,128)}, u32[]{:S(2)}) copy-start(f32[1,8,512,128]{3,2,1,0:T(8,128)} %get-tuple-element.316) | copy-start | bytes 6291460 | tf_op jit(solution)/shard_map/while/body/eval_jaxpr/cond
  49.1 5.0 %copy-start.25 = (bf16[512,1,128]{2,0,1:T(8,128)(2,1)S(1)}, bf16[512,1,128]{2,0,1:T(8,128)(2,1)}, u32[]{:S(2)}) copy-start(bf16[512,1,128]{2,0,1:T(8,128)(2,1)} %get-tuple-element.317) | copy-start | bytes 393220 | tf_op jit(solution)/shard_map/while/body/eval_jaxpr/cond
  57.2 1.3 copy-start.2
  74.0 6.0 %copy-start.21 = (s32[1,128,8]{1,2,0:T(8,128)S(1)}, s32[1,128,8]{1,2,0:T(8,128)}, u32[]{:S(2)}) copy-start(s32[1,128,8]{1,2,0:T(8,128)} %param.29) | copy-start | bytes 12292
  74.0 77.3 %copy-start.20 = (f32[2048]{0:T(1024)S(1)}, f32[2048]{0:T(1024)}, u32[]{:S(2)}) copy-start(f32[2048]{0:T(1024)} %param.28) | copy-start | bytes 24580
  154.3 144.5 %copy-start.23 = (bf16[1,2048,768]{2,1,0:T(8,128)(2,1)S(1)}, bf16[1,2048,768]{2,1,0:T(8,128)(2,1)}, u32[]{:S(2)}) copy-start(bf16[1,2048,768]{2,1,0:T(8,128)(2,1)} %param.31) | copy-start | bytes 9437188
  298.8 5.2 %copy-start.24 = (bf16[1,2048,768]{2,1,0:T(8,128)(2,1)S(1)}, bf16[1,2048,768]{2,1,0:T(8,128)(2,1)}, u32[]{:S(2)}) copy-start(bf16[1,2048,768]{2,1,0:T(8,128)(2,1)} %param.32) | copy-start | bytes 9437188
  316.7 4.1 copy-start.22
  316.7 143.9 %all-to-all-start.1 = ((bf16[32,48,2048]{2,1,0:T(8,128)(2,1)}), bf16[32,48,2048]{2,1,0:T(8,128)(2,1)}, u32[]{:S(2)}, u32[]{:S(2)}) async-start(bf16[32,48,2048]{2,1,0:T(8,128)(2,1)} %bitcast.359), calls=%async_computation.2 | async-start | bytes 12582912 | tf_op jit(solution)/shard_map/all_to_all | solution.py:146
Sparse Core Ops, SparseCore 0:
  80.1 69.9 reduce-scatter.1
where the time goes:
time: 491 us; the launch traced here: 489 us
  waiting for transfers between devices  194 us (40%)
  blocking collectives  144 us (29%)
  other arithmetic  36.4 us (7%)
  matrix products  32.7 us (7%)
  starting transfers between devices  30.1 us (6%)
  local copies, waits for them, and re-layouts  22.2 us (5%)
  between operations  17.7 us (4%)
  loops' own time  10.7 us (2%)
    all_to_all x1, blocking collectives, shards(): lax.all_to_all(outgoing, ('grp', 'dev'), split_axis=0, concat_axis=0, til...  144 us
    all_to_all x1, waiting for transfers between devices, shards(): lax.all_to_all(produced, ('grp', 'dev'), split_axis=0, concat_axis=0, til...  140 us
    reduce_scatter x1, waiting for transfers between devices, shards(): lax.psum_scatter(jnp.dot(attended, out_weight, preferred_element_type=jnp...  54.5 us
    ppermute x10, starting transfers between devices, shifted(): lax.ppermute(value, axis, [(source, source + steps) for source in range(l...  26.1 us
    gather x1, local copies, waits for them, and re-layouts, shards(): returned[target].reshape(dev_rows, top_count, model_width)  12.4 us
    another operation x6, loops' own time, one_step(): return lax.cond(jnp.any(allowed), update, lambda current: current, running)  10.7 us
  transfers between devices with their start and end apart: 12, of which 2 were waited for; matrix products, arithmetic and copies ran while one was open for 7% of the time, Pallas kernels for 0%

commit v1 on v0

v1 whole, which is shorter than its diff:
```python
import functools
import math

import jax
import jax.numpy as jnp
from jax import lax
from jax.experimental import pallas as pl
from jax.experimental.pallas import tpu as pltpu
from jax.sharding import PartitionSpec as P

HEAD_SIZE = 128
KEY_BLOCK = 256
FF_TILE = 256
VMEM_BYTES = 56 * 1024 * 1024
LOW = -1e30


def after(value, *others):
    return lax.optimization_barrier((value, *others))[0]


def swap_x(value):
    return lax.ppermute(value, "grp", [(i, i ^ 1) for i in range(lax.axis_size("grp"))])


def swap_y(value):
    return lax.ppermute(value, "grp", [(i, i ^ 2) for i in range(lax.axis_size("grp"))])


def swap_core(value):
    return lax.ppermute(value, "dev", [(i, i ^ 1) for i in range(lax.axis_size("dev"))])


def turn(value, planes):
    count = lax.axis_size("dev")
    return lax.ppermute(value, "dev", [(i, (i - 2 * planes) % count) for i in range(count)])


def earlier(value, steps, sources=lambda source: True):
    count = lax.axis_size("dev")
    pairs = [(i, i + steps) for i in range(count - steps) if sources(i)]
    return lax.ppermute(value, "dev", pairs)


def gather_keys(keys, values, reach):
    core = lax.axis_index("dev") % 2
    own = jnp.concatenate([keys, values], axis=1)
    whole = reach // 2
    lanes = [own] + [earlier(own, 2 * j) for j in range(1, whole + 1)]
    others = [swap_core(lane) for lane in lanes]
    pieces = []
    for j in range(whole + 1):
        first = jnp.where(core == 0, lanes[j], others[j])
        second = jnp.where(core == 0, others[j], lanes[j])
        pieces = [first, second] + pieces
    if reach % 2:
        pieces = [earlier(own, reach, lambda source: source % 2 == 1)] + pieces
    return jnp.concatenate(pieces, axis=0), len(pieces) - 2


def attend_kernel(place, q_ref, kv_ref, start_ref, out_ref, q_all, top, total):
    rows = q_ref.shape[0]
    heads = q_ref.shape[1] // HEAD_SIZE
    for h in range(heads):
        q_all[h * rows : (h + 1) * rows, :] = q_ref[:, h * HEAD_SIZE : (h + 1) * HEAD_SIZE]
    top[...] = jnp.full_like(top, LOW)
    total[...] = jnp.zeros_like(total)
    q_low, first_start, last_start = place[1], place[2], place[3]
    factor = math.log2(math.e) / math.sqrt(HEAD_SIZE)

    def step(block, masked):
        low = pl.multiple_of(block * KEY_BLOCK, KEY_BLOCK)
        key = kv_ref[pl.ds(low, KEY_BLOCK), :HEAD_SIZE]
        value = kv_ref[pl.ds(low, KEY_BLOCK), HEAD_SIZE:]
        value = jnp.concatenate([value, jnp.ones_like(value)], axis=1)
        score = lax.dot_general(
            q_all[...], key, (((1,), (1,)), ((), ())), preferred_element_type=jnp.float32
        )
        score = score * factor
        if masked:
            key_pos = low + lax.broadcasted_iota(jnp.int32, (rows, KEY_BLOCK), 1)
            q_pos = q_low + lax.broadcasted_iota(jnp.int32, (rows, KEY_BLOCK), 0)
            seen = (key_pos >= start_ref[...]) & (key_pos <= q_pos)
            score = jnp.where(seen[None], score.reshape(heads, rows, KEY_BLOCK), LOW)
            score = score.reshape(heads * rows, KEY_BLOCK)
        old = top[...]
        new = jnp.maximum(old, jnp.max(score, axis=1, keepdims=True))
        weight = jnp.exp2(score - jnp.concatenate([new] * (KEY_BLOCK // HEAD_SIZE), axis=1))
        shrink = jnp.exp2(old - new)
        added = jnp.dot(weight.astype(jnp.bfloat16), value, preferred_element_type=jnp.float32)
        total[...] = total[...] * jnp.concatenate([shrink, shrink], axis=1) + added
        top[...] = new

    def loop(low, high, masked):
        def body(block, carry):
            step(block, masked)
            return carry

        lax.fori_loop(low, high, body, 0)

    begin = first_start // KEY_BLOCK
    end = (q_low + rows - 1) // KEY_BLOCK + 1
    inner_low = jnp.minimum((last_start + KEY_BLOCK - 1) // KEY_BLOCK, end)
    inner_high = jnp.maximum((q_low + 1) // KEY_BLOCK, inner_low)
    loop(begin, inner_low, True)
    loop(inner_low, inner_high, False)
    loop(inner_high, end, True)
    for h in range(heads):
        part = total[h * rows : (h + 1) * rows, :]
        out_ref[:, h * HEAD_SIZE : (h + 1) * HEAD_SIZE] = (
            part[:, :HEAD_SIZE] / part[:, HEAD_SIZE:]
        ).astype(out_ref.dtype)


def attend(block, queries, key_values, starts, own_low, rows):
    width = queries.shape[1]
    heads = width // HEAD_SIZE
    mine = lax.dynamic_slice_in_dim(starts, block * rows, rows, 0)
    place = jnp.stack([block, own_low + block * rows, mine[0], mine[rows - 1]]).astype(jnp.int32)
    pairs = heads * rows * key_values.shape[0] // 2
    return pl.pallas_call(
        attend_kernel,
        grid_spec=pltpu.PrefetchScalarGridSpec(
            num_scalar_prefetch=1,
            grid=(1,),
            in_specs=[
                pl.BlockSpec((rows, width), lambda i, place: (place[0], 0)),
                pl.BlockSpec(key_values.shape, lambda i, place: (0, 0)),
                pl.BlockSpec((rows, 1), lambda i, place: (place[0], 0)),
            ],
            out_specs=pl.BlockSpec((rows, width), lambda i, place: (0, 0)),
            scratch_shapes=[
                pltpu.VMEM((heads * rows, HEAD_SIZE), jnp.bfloat16),
                pltpu.VMEM((heads * rows, HEAD_SIZE), jnp.float32),
                pltpu.VMEM((heads * rows, 2 * HEAD_SIZE), jnp.float32),
            ],
        ),
        out_shape=jax.ShapeDtypeStruct((rows, width), jnp.bfloat16),
        compiler_params=pltpu.CompilerParams(vmem_limit_bytes=VMEM_BYTES),
        cost_estimate=pl.CostEstimate(
            flops=4 * pairs * HEAD_SIZE, bytes_accessed=4 * key_values.size, transcendentals=pairs
        ),
        name="attend",
    )(place, queries, key_values, starts[:, None])


def expert_kernel(own, by_x, by_y, far_a, far_b, pick, share, g0, u0, d0, g1, u1, d1,
                  out_own, out_x, out_y, out_a, out_b, taken, summed, given):
    step = pl.program_id(0)
    tiles = pl.num_programs(0) // 2
    slots = pick.shape[1] // 2
    half = far_a.shape[0]

    @pl.when(step == 0)
    def _():
        for b, block in enumerate((own, by_x, by_y, None)):
            if block is not None:
                rows = jnp.dot(pick[b], block[...], preferred_element_type=jnp.float32)
            else:
                rows = jnp.dot(pick[b, :, :half], far_a[...], preferred_element_type=jnp.float32)
                rows += jnp.dot(pick[b, :, half:], far_b[...], preferred_element_type=jnp.float32)
            rows = rows.astype(taken.dtype)
            for e in range(2):
                taken[e, b * slots : (b + 1) * slots, :] = rows[e * slots : (e + 1) * slots]

    def tile(e, gate_ref, up_ref, down_ref):
        rows = taken[e]
        gate = jnp.dot(rows, gate_ref[...], preferred_element_type=jnp.float32)
        up = jnp.dot(rows, up_ref[...], preferred_element_type=jnp.float32)
        hidden = (gate / (1.0 + jnp.exp(-gate)) * up).astype(jnp.bfloat16)
        part = jnp.dot(hidden, down_ref[...], preferred_element_type=jnp.float32)
        at = step - e * tiles

        @pl.when(at == 0)
        def _():
            summed[...] = part

        @pl.when(at > 0)
        def _():
            summed[...] += part

        @pl.when(at == tiles - 1)
        def _():
            given[e] = (summed[...] * share[e]).astype(given.dtype)

    @pl.when(step < tiles)
    def _():
        tile(0, g0, u0, d0)

    @pl.when(step >= tiles)
    def _():
        tile(1, g1, u1, d1)

    @pl.when(step == 2 * tiles - 1)
    def _():
        for b, block in enumerate((out_own, out_x, out_y, None)):
            rows = jnp.concatenate([given[e, b * slots : (b + 1) * slots, :] for e in range(2)])
            back = lax.dot_general(
                pick[b], rows, (((0,), (0,)), ((), ())), preferred_element_type=jnp.float32
            ).astype(jnp.bfloat16)
            if block is not None:
                block[...] = back
            else:
                out_a[...] = back[:half]
                out_b[...] = back[half:]


def run_experts(blocks, pick, share, own_weights, other_weights):
    rows, width = blocks[0].shape
    half = blocks[3].shape[0]
    ff = own_weights[0].shape[1]
    tile = math.gcd(ff, FF_TILE)
    tiles = ff // tile
    slots = share.shape[1]

    def whole(shape):
        return pl.BlockSpec(shape, lambda i: (0,) * len(shape))

    def first(i):
        return jnp.minimum(i, tiles - 1)

    def second(i):
        return jnp.maximum(i - tiles, 0)

    weights = []
    for at in (first, second):
        weights += [
            pl.BlockSpec((width, tile), lambda i, at=at: (0, at(i))),
            pl.BlockSpec((width, tile), lambda i, at=at: (0, at(i))),
            pl.BlockSpec((tile, width), lambda i, at=at: (at(i), 0)),
        ]
    shapes = [(rows, width)] * 3 + [(half, width), (rows - half, width)]
    return pl.pallas_call(
        expert_kernel,
        grid=(2 * tiles,),
        in_specs=[whole(s) for s in shapes] + [whole(pick.shape), whole(share.shape)] + weights,
        out_specs=[whole(s) for s in shapes],
        out_shape=[jax.ShapeDtypeStruct(s, jnp.bfloat16) for s in shapes],
        scratch_shapes=[
            pltpu.VMEM((2, slots, width), jnp.bfloat16),
            pltpu.VMEM((slots, width), jnp.float32),
            pltpu.VMEM((2, slots, width), jnp.bfloat16),
        ],
        compiler_params=pltpu.CompilerParams(vmem_limit_bytes=VMEM_BYTES),
        cost_estimate=pl.CostEstimate(
            flops=12 * slots * width * ff,
            bytes_accessed=12 * width * ff + 16 * rows * width,
            transcendentals=2 * slots * ff,
        ),
        name="experts",
    )(*blocks, pick, share, *own_weights, *other_weights)


def spread(block):
    half = block.shape[0] // 2
    by_x, by_y = swap_x(block), swap_y(block)
    return block, by_x, by_y, swap_y(by_x[:half]), swap_x(by_y[half:])


def collect(own, by_x, by_y, far_a, far_b):
    half = far_a.shape[0]
    from_a, from_b = swap_x(far_a), swap_y(far_b)
    by_y = jnp.concatenate([by_y[:half] + from_a, by_y[half:]])
    by_x = jnp.concatenate([by_x[:half], by_x[half:] + from_b])
    return own.astype(jnp.float32) + swap_x(by_x).astype(jnp.float32) + swap_y(by_y).astype(jnp.float32)


def routing(ids, gates, expert_count, slots):
    dev_size = lax.axis_size("dev")
    planes = dev_size // 2
    dense = jnp.sum(
        jnp.where(
            ids.T[None] == jnp.arange(expert_count, dtype=jnp.int32)[:, None, None], gates.T[None], 0.0
        ),
        axis=1,
    )
    pair = jnp.stack([dense, swap_x(dense)])
    four = jnp.concatenate([pair, swap_y(pair)])
    every = jnp.stack([four] + [turn(four, k) for k in range(1, planes)])
    me = lax.axis_index("grp") * dev_size + lax.axis_index("dev")
    mine = jnp.stack(
        [lax.dynamic_index_in_dim(every, e, 2, keepdims=False) for e in (me, me ^ 1)], axis=2
    )
    named = mine > 0
    tokens = mine.shape[-1]
    before = jnp.triu(jnp.ones((tokens, tokens), jnp.bfloat16), 1)
    rank = jnp.dot(named.astype(jnp.bfloat16), before, preferred_element_type=jnp.float32)
    slot = jnp.arange(slots, dtype=jnp.int32).astype(jnp.float32)
    chosen = named[..., None, :] & (rank[..., None, :] == slot[:, None])
    share = jnp.sum(jnp.where(chosen, mine[..., None, :], 0.0), axis=-1)
    pick = chosen.astype(jnp.bfloat16).reshape(planes, 4, 2 * slots, tokens)
    share = share.transpose(0, 2, 1, 3).reshape(planes, 2, 4 * slots, 1)
    return pick, share


def shards(
    queries,
    keys,
    values,
    doc_ids,
    out_weight,
    norm_gain,
    expert_ids,
    gate_values,
    expert_gate,
    expert_up,
    expert_down,
):
    own_rows = queries.shape[0]
    grp_size = lax.axis_size("grp")
    dev_size = lax.axis_size("dev")
    planes = dev_size // 2
    group, device = lax.axis_index("grp"), lax.axis_index("dev")
    dev_rows = own_rows // grp_size
    width = out_weight.shape[1]
    top_count = expert_ids.shape[2]
    expert_count = grp_size * dev_size
    capacity = max(2, 3 * dev_rows * top_count // (2 * expert_count))
    slots = -(-capacity // 16) * 16
    doc_reach = dev_size * own_rows // 2 + own_rows
    reach = min(dev_size - 1, (doc_reach + own_rows - 1) // own_rows)

    key_values, ahead = gather_keys(keys, values, reach)
    own_low = (ahead + device % 2) * own_rows
    own_docs = lax.dynamic_slice_in_dim(doc_ids, device * own_rows, own_rows, 0)
    starts = jnp.sum((doc_ids[None, :] < own_docs[:, None]).astype(jnp.int32), axis=1)
    starts = starts - device * own_rows + own_low

    pick, share = routing(expert_ids[0], gate_values[0], expert_count, slots)
    own_weights = [expert_gate[0], expert_up[0], expert_down[0]]

    def part(block):
        attended = attend(block, queries, key_values, starts, own_low, dev_rows)
        return jnp.dot(attended, out_weight, preferred_element_type=jnp.float32)

    half = dev_rows // 2
    far = part(group ^ 3).astype(jnp.bfloat16)
    by_x = part(group ^ 1).astype(jnp.bfloat16)
    by_y = part(group ^ 2).astype(jnp.bfloat16)
    own = part(group)
    projected = collect(own, by_x, by_y, far[:half], far[half:])
    other_weights = [swap_core(after(w, far)) for w in own_weights]
    normed = (
        projected
        * lax.rsqrt(jnp.mean(projected * projected, axis=-1, keepdims=True) + 1e-06)
        * norm_gain
    ).astype(jnp.bfloat16)

    order = sorted(range(1, planes), key=lambda k: min(k, planes - k))
    turned, last = {0: normed}, normed
    for k in order:
        last = turned[k] = turn(after(normed, last), k)
    results = {}
    for k in [0] + order:
        results[k] = run_experts(spread(turned[k]), pick[k], share[k], own_weights, other_weights)
    mixed = 0.0
    for k in list(range(1, planes)) + [0]:
        summed = collect(*results[k])
        if k:
            summed = turn(summed.astype(jnp.bfloat16), planes - k).astype(jnp.float32)
        mixed = mixed + summed
    return (projected + mixed).astype(jnp.bfloat16)[None]


def solution(mesh):
    return jax.shard_map(
        shards,
        mesh=mesh,
        in_specs=(
            P("dev", "grp"),
            P("dev", "grp"),
            P("dev", "grp"),
            P(),
            P("grp", None),
            P(),
            P("dev", "grp", None),
            P("dev", "grp", None),
            P(("grp", "dev"), None, None),
            P(("grp", "dev"), None, None),
            P(("grp", "dev"), None, None),
        ),
        out_specs=P("dev", "grp", None),
        check_vma=False,
    )
```

time: 491 us -> 339 us (0.69)
  blocking collectives: 144 us -> 0 us
  Pallas kernels: 0 us -> 77 us
  waiting for transfers between devices: 194 us -> 131 us
  starting transfers between devices: 30.1 us -> 83.2 us
  matrix products: 32.7 us -> 8.64 us
  other arithmetic: 36.4 us -> 16.3 us
  between operations: 17.7 us -> 0.72 us
  loops' own time: 10.7 us -> 0 us
    all_to_all x1 -> x0, blocking collectives: 144 us -> none  [shards(): lax.all_to_all(outgoing, ('grp', 'dev'), split_axis=0, concat_axis=0, til...]
    all_to_all x1 -> x0, waiting for transfers between devices: 140 us -> none  [shards(): lax.all_to_all(produced, ('grp', 'dev'), split_axis=0, concat_axis=0, til...]
    ppermute x10 -> x56, waiting for transfers between devices: 0.03 us -> 131 us  [the longest x19 52.6 us: swap_x(): lax.ppermute(value, 'grp', [(i, i ^ 1) for i in range(lax.axis_size('grp'...]
    pallas_call x0 -> x8, Pallas kernels: none -> 77 us  [the longest x4 61.3 us: run_experts(): pl.pallas_call(expert_kernel, grid=(2 * tiles,), in_specs=[whole(s) for s...]
    ppermute x10 -> x56, starting transfers between devices: 26.1 us -> 83.2 us  [the longest x9 24.2 us: turn(): lax.ppermute(value, 'dev', [(i, (i - 2 * planes) % count) for i in range(...]
    reduce_scatter x1 -> x0, waiting for transfers between devices: 54.5 us -> none  [shards(): lax.psum_scatter(jnp.dot(attended, out_weight, preferred_element_type=jnp...]
    dot_general x7 -> x5, matrix products: 32.7 us -> 8.64 us  [the longest x4 8.5 us: part(): return jnp.dot(attended, out_weight, preferred_element_type=jnp.float32)]
    gather x1 -> x0, local copies, waits for them, and re-layouts: 12.4 us -> none  [shards(): returned[target].reshape(dev_rows, top_count, model_width)]
  transfers between devices with their start and end apart: 12 -> 56, of which waited for: 2 -> 23; matrix products, arithmetic and copies ran while one was open for 7% -> 10% of each run, Pallas kernels for 0% -> 22%
where the time goes in v1:
time: 339 us; the launch traced here: 336 us
  waiting for transfers between devices  131 us (39%)
  starting transfers between devices  83.2 us (25%)
  Pallas kernels  77 us (23%)
  local copies, waits for them, and re-layouts  19.5 us (6%)
  other arithmetic  16.3 us (5%)
  matrix products  8.64 us (3%)
    pallas_call x4, Pallas kernels, run_experts(): pl.pallas_call(expert_kernel, grid=(2 * tiles,), in_specs=[whole(s) for s...  61.3 us
    ppermute x19, waiting for transfers between devices, swap_x(): lax.ppermute(value, 'grp', [(i, i ^ 1) for i in range(lax.axis_size('grp'...  52.6 us
    ppermute x19, waiting for transfers between devices, swap_y(): lax.ppermute(value, 'grp', [(i, i ^ 2) for i in range(lax.axis_size('grp'...  43.4 us
    ppermute x9, waiting for transfers between devices, turn(): lax.ppermute(value, 'dev', [(i, (i - 2 * planes) % count) for i in range(...  33.4 us
    ppermute x9, starting transfers between devices, turn(): lax.ppermute(value, 'dev', [(i, (i - 2 * planes) % count) for i in range(...  24.2 us
    ppermute x19, starting transfers between devices, swap_x(): lax.ppermute(value, 'grp', [(i, i ^ 1) for i in range(lax.axis_size('grp'...  23.5 us
    ppermute x19, starting transfers between devices, swap_y(): lax.ppermute(value, 'grp', [(i, i ^ 2) for i in range(lax.axis_size('grp'...  21.3 us
    pallas_call x4, Pallas kernels, attend(): pl.pallas_call(attend_kernel, grid_spec=pltpu.PrefetchScalarGridSpec(num_...  15.7 us
  transfers between devices with their start and end apart: 56, of which 23 were waited for; matrix products, arithmetic and copies ran while one was open for 10% of the time, Pallas kernels for 22%

profile of v1, /device:TPU:0, one launch (start us, length us, event | category | flops | bytes accessed | tf_op | source)
XLA Modules:
  0.0 336.0 jit_solution(7606635427168732494)
XLA Ops:
  1.9 6.0 %collective-permute-start.1 = (bf16[512,256]{1,0:T(8,128)(2,1)S(1)}, bf16[512,256]{1,0:T(8,128)(2,1)S(1)}, u32[]{:S(2)}, u32[]{:S(2)}) collective-permute-start(bf16[512,256]{1,0:T(8,128)(2,1)S(1)} %constant_dynamic-update-slice_fusion), channel_id=1, source_target_pairs={{0,4},{1,5},{2,6},{3,7},{8,12},{9,13},{10,14},{11,15},{16,20},{17,... | collective-permute-start | bytes 786440 | tf_op jit(solution)/shard_map/ppermute | solution.py:42
  8.5 3.5 %collective-permute-start.3 = (bf16[512,256]{1,0:T(8,128)(2,1)S(1)}, bf16[512,256]{1,0:T(8,128)(2,1)S(1)}, u32[]{:S(2)}, u32[]{:S(2)}) collective-permute-start(bf16[512,256]{1,0:T(8,128)(2,1)S(1)} %constant_dynamic-update-slice_fusion), channel_id=1, source_target_pairs={{0,2},{1,3},{2,4},{3,5},{4,6},{5,7},{8,10},{9,11},{10,12},{11,13},... | collective-permute-start | bytes 786440 | tf_op jit(solution)/shard_map/ppermute | solution.py:42
  26.2 3.7 %attend.6 = bf16[128,1024]{1,0:T(8,128)(2,1)} custom-call(s32[4]{0:T(128)} %pad_add_fusion.2.place, bf16[512,1024]{1,0:T(8,128)(2,1)} %q_ref.7, bf16[3584,256]{1,0:T(8,128)(2,1)} %copy-done.22, s32[512,1]{1,0:T(8,128)} %copy.47.start_ref), custom_call_target="tpu_custom_call" | custom-call | flops 939524096 | bytes 3670016 | tf_op jit(solution)/shard_map/attend/pallas_call | solution.py:121
  33.2 3.7 %attend.5 = bf16[128,1024]{1,0:T(8,128)(2,1)} custom-call(s32[4]{0:T(128)} %pad_add_fusion.1.place, bf16[512,1024]{1,0:T(8,128)(2,1)} %q_ref.7, bf16[3584,256]{1,0:T(8,128)(2,1)} %copy-done.22, s32[512,1]{1,0:T(8,128)} %copy.47.start_ref), custom_call_target="tpu_custom_call" | custom-call | flops 939524096 | bytes 3670016 | tf_op jit(solution)/shard_map/attend/pallas_call | solution.py:121
  40.1 4.4 %attend.7 = bf16[128,1024]{1,0:T(8,128)(2,1)} custom-call(s32[4]{0:T(128)} %pad_add_fusion.3.place, bf16[512,1024]{1,0:T(8,128)(2,1)} %q_ref.7, bf16[3584,256]{1,0:T(8,128)(2,1)} %copy-done.22, s32[512,1]{1,0:T(8,128)} %copy.47.start_ref), custom_call_target="tpu_custom_call" | custom-call | flops 939524096 | bytes 3670016 | tf_op jit(solution)/shard_map/attend/pallas_call | solution.py:121
  51.4 3.9 %attend.4 = bf16[128,1024]{1,0:T(8,128)(2,1)} custom-call(s32[4]{0:T(128)} %pad_add_fusion.place, bf16[512,1024]{1,0:T(8,128)(2,1)} %q_ref.7, bf16[3584,256]{1,0:T(8,128)(2,1)} %copy-done.22, s32[512,1]{1,0:T(8,128)} %copy.47.start_ref), custom_call_target="tpu_custom_call" | custom-call | flops 939524096 | bytes 3670016 | tf_op jit(solution)/shard_map/attend/pallas_call | solution.py:121
  55.3 6.5 %collective-permute-done.7 = bf16[128,2048]{1,0:T(8,128)(2,1)} collective-permute-done((bf16[128,2048]{1,0:T(8,128)(2,1)}, bf16[128,2048]{1,0:T(8,128)(2,1)}, u32[]{:S(2)}, u32[]{:S(2)}) %collective-permute-start.7) | collective-permute-done | bytes 524320 | tf_op jit(solution)/shard_map/ppermute | solution.py:23
  63.5 3.5 %multiply_reduce_fusion = (f32[128]{0:T(128)S(1)}, f32[128,2048]{1,0:T(8,128)S(1)}) fusion(bf16[128,2048]{1,0:T(8,128)(2,1)} %collective-permute-done.9, bf16[128,2048]{1,0:T(8,128)(2,1)} %collective-permute-done.7, bf16[128,1024]{1,0:T(8,128)(2,1)} %attend.4, bf16[1024,2048]{1,0:T(8,128)(2,1)} %param.15), kind=kOutput, calls=%fused_computation.11 | convolution fusion | flops 538443648 | bytes 6554112 | tf_op jit(solution)/shard_map/dot_general | solution.py:334
  68.1 8.8 %collective-permute-start.10 = (bf16[128,2048]{1,0:T(8,128)(2,1)}, bf16[128,2048]{1,0:T(8,128)(2,1)}, u32[]{:S(2)}, u32[]{:S(2)}) collective-permute-start(bf16[128,2048]{1,0:T(8,128)(2,1)} %multiply_convert_fusion.own), channel_id=1, source_target_pairs={{0,6},{1,7},{2,0},{3,1},{4,2},{5,3},{6,4},{7,5},{8,14},{9,15},{10,... | collective-permute-start | bytes 1572872 | tf_op jit(solution)/shard_map/ppermute | solution.py:36
  81.4 3.4 %collective-permute-done.16 = f32[2,32,128]{2,0,1:T(2,128)S(1)} collective-permute-done((f32[2,32,128]{2,0,1:T(2,128)S(1)}, f32[2,32,128]{2,0,1:T(2,128)S(1)}, u32[]{:S(2)}, u32[]{:S(2)}) %collective-permute-start.16) | collective-permute-done | bytes 32800 | tf_op jit(solution)/shard_map/ppermute | solution.py:27
  84.8 11.8 %collective-permute-start.17 = (f32[4,32,128]{2,0,1:T(4,128)S(1)}, f32[4,32,128]{2,0,1:T(4,128)S(1)}, u32[]{:S(2)}, u32[]{:S(2)}) collective-permute-start(f32[4,32,128]{2,0,1:T(4,128)S(1)} %get-tuple-element.86), channel_id=1, source_target_pairs={{0,6},{1,7},{2,0},{3,1},{4,2},{5,3},{6,4},{7,5},{8,14},{9,15},{10,... | collective-permute-start | bytes 196616 | tf_op jit(solution)/shard_map/ppermute | solution.py:36
  98.8 2.8 collective-permute-start.28
  104.2 3.3 collective-permute-start.22
  107.4 4.5 %collective-permute-done.48.by_x = bf16[128,2048]{1,0:T(8,128)(2,1)} collective-permute-done((bf16[128,2048]{1,0:T(8,128)(2,1)}, bf16[128,2048]{1,0:T(8,128)(2,1)}, u32[]{:S(2)}, u32[]{:S(2)}) %collective-permute-start.48) | collective-permute-done | bytes 524320 | tf_op jit(solution)/shard_map/ppermute | solution.py:23
  113.4 2.3 collective-permute-done.28.own
  116.7 9.2 %collective-permute-done.49.by_y = bf16[128,2048]{1,0:T(8,128)(2,1)} collective-permute-done((bf16[128,2048]{1,0:T(8,128)(2,1)}, bf16[128,2048]{1,0:T(8,128)(2,1)}, u32[]{:S(2)}, u32[]{:S(2)}) %collective-permute-start.49) | collective-permute-done | bytes 524320 | tf_op jit(solution)/shard_map/ppermute | solution.py:27
  127.6 3.0 collective-permute-done.11.by_x
  130.6 8.6 %collective-permute-done.12.by_y = bf16[128,2048]{1,0:T(8,128)(2,1)} collective-permute-done((bf16[128,2048]{1,0:T(8,128)(2,1)}, bf16[128,2048]{1,0:T(8,128)(2,1)}, u32[]{:S(2)}, u32[]{:S(2)}) %collective-permute-start.12) | collective-permute-done | bytes 524320 | tf_op jit(solution)/shard_map/ppermute | solution.py:27
  140.6 14.1 %collective-permute-done.29.own = bf16[128,2048]{1,0:T(8,128)(2,1)} collective-permute-done((bf16[128,2048]{1,0:T(8,128)(2,1)}, bf16[128,2048]{1,0:T(8,128)(2,1)}, u32[]{:S(2)}, u32[]{:S(2)}) %collective-permute-start.29) | collective-permute-done | bytes 524320 | tf_op jit(solution)/shard_map/ppermute | solution.py:36
  157.7 11.2 %collective-permute-done.40.by_y = bf16[128,2048]{1,0:T(8,128)(2,1)} collective-permute-done((bf16[128,2048]{1,0:T(8,128)(2,1)}, bf16[128,2048]{1,0:T(8,128)(2,1)}, u32[]{:S(2)}, u32[]{:S(2)}) %collective-permute-start.40) | collective-permute-done | bytes 524320 | tf_op jit(solution)/shard_map/ppermute | solution.py:27
  175.1 9.0 %collective-permute-done.31.by_y = bf16[128,2048]{1,0:T(8,128)(2,1)} collective-permute-done((bf16[128,2048]{1,0:T(8,128)(2,1)}, bf16[128,2048]{1,0:T(8,128)(2,1)}, u32[]{:S(2)}, u32[]{:S(2)}) %collective-permute-start.31) | collective-permute-done | bytes 524320 | tf_op jit(solution)/shard_map/ppermute | solution.py:27
  200.9 15.3 %experts.4 = (bf16[128,2048]{1,0:T(8,128)(2,1)}, bf16[128,2048]{1,0:T(8,128)(2,1)}, bf16[128,2048]{1,0:T(8,128)(2,1)}, bf16[64,2048]{1,0:T(8,128)(2,1)}, bf16[64,2048]{1,0:T(8,128)(2,1)}) custom-call(bf16[128,2048]{1,0:T(8,128)(2,1)} %collective-permute-done.10.own, bf16[128,2048]{1,0:T(8,128)(2,1)} %collective-permute-done.11.by_x, ...), custom_call_target="tpu_custom_call" | custom-call | flops 3623878656 | bytes 23068672 | tf_op jit(solution)/shard_map/experts/pallas_call | solution.py:233
  217.5 15.2 %experts.5 = (bf16[128,2048]{1,0:T(8,128)(2,1)}, bf16[128,2048]{1,0:T(8,128)(2,1)}, bf16[128,2048]{1,0:T(8,128)(2,1)}, bf16[64,2048]{1,0:T(8,128)(2,1)}, bf16[64,2048]{1,0:T(8,128)(2,1)}) custom-call(bf16[128,2048]{1,0:T(8,128)(2,1)} %collective-permute-done.29.own, bf16[128,2048]{1,0:T(8,128)(2,1)} %collective-permute-done.30.by_x, ...), custom_call_target="tpu_custom_call" | custom-call | flops 3623878656 | bytes 23068672 | tf_op jit(solution)/shard_map/experts/pallas_call | solution.py:233
  235.6 15.2 %experts.6 = (bf16[128,2048]{1,0:T(8,128)(2,1)}, bf16[128,2048]{1,0:T(8,128)(2,1)}, bf16[128,2048]{1,0:T(8,128)(2,1)}, bf16[64,2048]{1,0:T(8,128)(2,1)}, bf16[64,2048]{1,0:T(8,128)(2,1)}) custom-call(bf16[128,2048]{1,0:T(8,128)(2,1)} %collective-permute-done.28.own, bf16[128,2048]{1,0:T(8,128)(2,1)} %collective-permute-done.39.by_x, ...), custom_call_target="tpu_custom_call" | custom-call | flops 3623878656 | bytes 23068672 | tf_op jit(solution)/shard_map/experts/pallas_call | solution.py:233
  252.2 15.5 %experts.7 = (bf16[128,2048]{1,0:T(8,128)(2,1)}, bf16[128,2048]{1,0:T(8,128)(2,1)}, bf16[128,2048]{1,0:T(8,128)(2,1)}, bf16[64,2048]{1,0:T(8,128)(2,1)}, bf16[64,2048]{1,0:T(8,128)(2,1)}) custom-call(bf16[128,2048]{1,0:T(8,128)(2,1)} %multiply_convert_fusion.own, bf16[128,2048]{1,0:T(8,128)(2,1)} %collective-permute-done.48.by_x, ...), custom_call_target="tpu_custom_call" | custom-call | flops 3623878656 | bytes 23068672 | tf_op jit(solution)/shard_map/experts/pallas_call | solution.py:233
  274.2 3.0 collective-permute-done.45
  280.4 2.4 collective-permute-done.54
  284.5 9.5 %collective-permute-done.24 = bf16[128,2048]{1,0:T(8,128)(2,1)S(1)} collective-permute-done((bf16[128,2048]{1,0:T(8,128)(2,1)S(1)}, bf16[128,2048]{1,0:T(8,128)(2,1)S(1)}, u32[]{:S(2)}, u32[]{:S(2)}) %collective-permute-start.24) | collective-permute-done | bytes 524320 | tf_op jit(solution)/shard_map/ppermute | solution.py:23
  297.0 8.2 %collective-permute-done.35 = bf16[128,2048]{1,0:T(8,128)(2,1)S(1)} collective-permute-done((bf16[128,2048]{1,0:T(8,128)(2,1)S(1)}, bf16[128,2048]{1,0:T(8,128)(2,1)S(1)}, u32[]{:S(2)}, u32[]{:S(2)}) %collective-permute-start.35) | collective-permute-done | bytes 524320 | tf_op jit(solution)/shard_map/ppermute | solution.py:23
  306.4 8.0 %collective-permute-done.44 = bf16[128,2048]{1,0:T(8,128)(2,1)S(1)} collective-permute-done((bf16[128,2048]{1,0:T(8,128)(2,1)S(1)}, bf16[128,2048]{1,0:T(8,128)(2,1)S(1)}, u32[]{:S(2)}, u32[]{:S(2)}) %collective-permute-start.44) | collective-permute-done | bytes 524320 | tf_op jit(solution)/shard_map/ppermute | solution.py:23
  314.8 5.2 %collective-permute-done.53 = bf16[128,2048]{1,0:T(8,128)(2,1)S(1)} collective-permute-done((bf16[128,2048]{1,0:T(8,128)(2,1)S(1)}, bf16[128,2048]{1,0:T(8,128)(2,1)S(1)}, u32[]{:S(2)}, u32[]{:S(2)}) %collective-permute-start.53) | collective-permute-done | bytes 524320 | tf_op jit(solution)/shard_map/ppermute | solution.py:23
  320.0 14.7 %collective-permute-done.38 = bf16[128,2048]{1,0:T(8,128)(2,1)S(1)} collective-permute-done((bf16[128,2048]{1,0:T(8,128)(2,1)S(1)}, bf16[128,2048]{1,0:T(8,128)(2,1)S(1)}, u32[]{:S(2)}, u32[]{:S(2)}) %collective-permute-start.38) | collective-permute-done | bytes 524320 | tf_op jit(solution)/shard_map/ppermute | solution.py:36
  (228 shorter events, 96.0 us)
Async XLA Ops:
  1.9 16.1 %collective-permute-start.1 = (bf16[512,256]{1,0:T(8,128)(2,1)S(1)}, bf16[512,256]{1,0:T(8,128)(2,1)S(1)}, u32[]{:S(2)}, u32[]{:S(2)}) collective-permute-start(bf16[512,256]{1,0:T(8,128)(2,1)S(1)} %constant_dynamic-update-slice_fusion), channel_id=1, source_target_pairs={{0,4},{1,5},{2,6},{3,7},{8,12},{9,13},{10,14},{11,15},{16,20},{17,... | collective-permute-start | bytes 786440 | tf_op jit(solution)/shard_map/ppermute | solution.py:42
  7.8 15.3 %collective-permute-start = (bf16[512,256]{1,0:T(8,128)(2,1)S(1)}, bf16[512,256]{1,0:T(8,128)(2,1)S(1)}, u32[]{:S(2)}, u32[]{:S(2)}) collective-permute-start(bf16[512,256]{1,0:T(8,128)(2,1)S(1)} %constant_dynamic-update-slice_fusion), channel_id=1, source_target_pairs={{1,6},{9,14},{17,22},{25,30}} | collective-permute-start | bytes 786440 | tf_op jit(solution)/shard_map/ppermute | solution.py:42
  68.1 30.6 %collective-permute-start.10 = (bf16[128,2048]{1,0:T(8,128)(2,1)}, bf16[128,2048]{1,0:T(8,128)(2,1)}, u32[]{:S(2)}, u32[]{:S(2)}) collective-permute-start(bf16[128,2048]{1,0:T(8,128)(2,1)} %multiply_convert_fusion.own), channel_id=1, source_target_pairs={{0,6},{1,7},{2,0},{3,1},{4,2},{5,3},{6,4},{7,5},{8,14},{9,15},{10,... | collective-permute-start | bytes 1572872 | tf_op jit(solution)/shard_map/ppermute | solution.py:36
  84.8 16.8 %collective-permute-start.17 = (f32[4,32,128]{2,0,1:T(4,128)S(1)}, f32[4,32,128]{2,0,1:T(4,128)S(1)}, u32[]{:S(2)}, u32[]{:S(2)}) collective-permute-start(f32[4,32,128]{2,0,1:T(4,128)S(1)} %get-tuple-element.86), channel_id=1, source_target_pairs={{0,6},{1,7},{2,0},{3,1},{4,2},{5,3},{6,4},{7,5},{8,14},{9,15},{10,... | collective-permute-start | bytes 196616 | tf_op jit(solution)/shard_map/ppermute | solution.py:36
  98.8 17.0 %collective-permute-start.28 = (bf16[128,2048]{1,0:T(8,128)(2,1)}, bf16[128,2048]{1,0:T(8,128)(2,1)}, u32[]{:S(2)}, u32[]{:S(2)}) collective-permute-start(bf16[128,2048]{1,0:T(8,128)(2,1)} %multiply_convert_fusion.own), channel_id=1, source_target_pairs={{0,2},{1,3},{2,4},{3,5},{4,6},{5,7},{6,0},{7,1},{8,10},{9,11},{10,... | collective-permute-start | bytes 1572872 | tf_op jit(solution)/shard_map/ppermute | solution.py:36
  101.6 95.3 %collective-permute-start.20 = (bf16[2048,768]{1,0:T(8,128)(2,1)S(1)}, bf16[2048,768]{1,0:T(8,128)(2,1)}, u32[]{:S(2)}, u32[]{:S(2)}) collective-permute-start(bf16[2048,768]{1,0:T(8,128)(2,1)S(1)} %bitcast.49), channel_id=1, source_target_pairs={{0,1},{1,0},{2,3},{3,2},{4,5},{5,4},{6,7},{7,6},{8,9},{9,8},{10,11... | collective-permute-start | bytes 9437192 | tf_op jit(solution)/shard_map/ppermute | solution.py:31
  103.9 94.1 %collective-permute-start.21 = (bf16[2048,768]{1,0:T(8,128)(2,1)}, bf16[2048,768]{1,0:T(8,128)(2,1)}, u32[]{:S(2)}, u32[]{:S(2)}) collective-permute-start(bf16[2048,768]{1,0:T(8,128)(2,1)} %bitcast.24.u0), channel_id=1, source_target_pairs={{0,1},{1,0},{2,3},{3,2},{4,5},{5,4},{6,7},{7,6},{8,9},{9,8},{10,11... | collective-permute-start | bytes 9437192 | tf_op jit(solution)/shard_map/ppermute | solution.py:31
  104.2 94.8 %collective-permute-start.22 = (bf16[768,2048]{1,0:T(8,128)(2,1)}, bf16[768,2048]{1,0:T(8,128)(2,1)}, u32[]{:S(2)}, u32[]{:S(2)}) collective-permute-start(bf16[768,2048]{1,0:T(8,128)(2,1)} %bitcast.25.d0), channel_id=1, source_target_pairs={{0,1},{1,0},{2,3},{3,2},{4,5},{5,4},{6,7},{7,6},{8,9},{9,8},{10,11... | collective-permute-start | bytes 9437192 | tf_op jit(solution)/shard_map/ppermute | solution.py:31
  130.6 24.1 %collective-permute-start.29 = (bf16[128,2048]{1,0:T(8,128)(2,1)}, bf16[128,2048]{1,0:T(8,128)(2,1)}, u32[]{:S(2)}, u32[]{:S(2)}) collective-permute-start(bf16[128,2048]{1,0:T(8,128)(2,1)} %multiply_convert_fusion.own), channel_id=1, source_target_pairs={{0,4},{1,5},{2,6},{3,7},{4,0},{5,1},{6,2},{7,3},{8,12},{9,13},{10,... | collective-permute-start | bytes 1572872 | tf_op jit(solution)/shard_map/ppermute | solution.py:36
  139.2 16.6 %collective-permute-start.39 = (bf16[128,2048]{1,0:T(8,128)(2,1)}, bf16[128,2048]{1,0:T(8,128)(2,1)}, u32[]{:S(2)}, u32[]{:S(2)}) collective-permute-start(bf16[128,2048]{1,0:T(8,128)(2,1)} %collective-permute-done.28.own), channel_id=1, source_target_pairs={{0,8},{8,0},{16,24},{24,16},{1,9},{9,1},{17,25},{25,17},{2,10},{10... | collective-permute-start | bytes 1572872 | tf_op jit(solution)/shard_map/ppermute | solution.py:23
  155.8 18.2 %collective-permute-start.30 = (bf16[128,2048]{1,0:T(8,128)(2,1)}, bf16[128,2048]{1,0:T(8,128)(2,1)}, u32[]{:S(2)}, u32[]{:S(2)}) collective-permute-start(bf16[128,2048]{1,0:T(8,128)(2,1)} %collective-permute-done.29.own), channel_id=1, source_target_pairs={{0,8},{8,0},{16,24},{24,16},{1,9},{9,1},{17,25},{25,17},{2,10},{10... | collective-permute-start | bytes 1572872 | tf_op jit(solution)/shard_map/ppermute | solution.py:23
  174.0 21.5 %collective-permute-start.13 = (bf16[64,2048]{1,0:T(8,128)(2,1)}, bf16[64,2048]{1,0:T(8,128)(2,1)}, u32[]{:S(2)}, u32[]{:S(2)}) collective-permute-start(bf16[64,2048]{1,0:T(8,128)(2,1)} %slice.198), channel_id=1, source_target_pairs={{0,16},{8,24},{16,0},{24,8},{1,17},{9,25},{17,1},{25,9},{2,18},{10... | collective-permute-start | bytes 786440 | tf_op jit(solution)/shard_map/ppermute | solution.py:27
  195.5 55.4 %collective-permute-start.50 = (bf16[64,2048]{1,0:T(8,128)(2,1)S(1)}, bf16[64,2048]{1,0:T(8,128)(2,1)S(1)}, u32[]{:S(2)}, u32[]{:S(2)}) collective-permute-start(bf16[64,2048]{1,0:T(8,128)(2,1)S(1)} %slice.210), channel_id=1, source_target_pairs={{0,16},{8,24},{16,0},{24,8},{1,17},{9,25},{17,1},{25,9},{2,18},{10... | collective-permute-start | bytes 786440 | tf_op jit(solution)/shard_map/ppermute | solution.py:27
  196.8 54.3 %collective-permute-start.51 = (bf16[64,2048]{1,0:T(8,128)(2,1)S(1)}, bf16[64,2048]{1,0:T(8,128)(2,1)S(1)}, u32[]{:S(2)}, u32[]{:S(2)}) collective-permute-start(bf16[64,2048]{1,0:T(8,128)(2,1)S(1)} %slice.211), channel_id=1, source_target_pairs={{0,8},{8,0},{16,24},{24,16},{1,9},{9,1},{17,25},{25,17},{2,10},{10... | collective-permute-start | bytes 786440 | tf_op jit(solution)/shard_map/ppermute | solution.py:23
  196.9 35.8 %collective-permute-start.41 = (bf16[64,2048]{1,0:T(8,128)(2,1)S(1)}, bf16[64,2048]{1,0:T(8,128)(2,1)S(1)}, u32[]{:S(2)}, u32[]{:S(2)}) collective-permute-start(bf16[64,2048]{1,0:T(8,128)(2,1)S(1)} %slice.206), channel_id=1, source_target_pairs={{0,16},{8,24},{16,0},{24,8},{1,17},{9,25},{17,1},{25,9},{2,18},{10... | collective-permute-start | bytes 786440 | tf_op jit(solution)/shard_map/ppermute | solution.py:27
  198.0 18.1 %collective-permute-start.32 = (bf16[64,2048]{1,0:T(8,128)(2,1)S(1)}, bf16[64,2048]{1,0:T(8,128)(2,1)S(1)}, u32[]{:S(2)}, u32[]{:S(2)}) collective-permute-start(bf16[64,2048]{1,0:T(8,128)(2,1)S(1)} %slice.202), channel_id=1, source_target_pairs={{0,16},{8,24},{16,0},{24,8},{1,17},{9,25},{17,1},{25,9},{2,18},{10... | collective-permute-start | bytes 786440 | tf_op jit(solution)/shard_map/ppermute | solution.py:27
  199.0 17.4 %collective-permute-start.33 = (bf16[64,2048]{1,0:T(8,128)(2,1)S(1)}, bf16[64,2048]{1,0:T(8,128)(2,1)S(1)}, u32[]{:S(2)}, u32[]{:S(2)}) collective-permute-start(bf16[64,2048]{1,0:T(8,128)(2,1)S(1)} %slice.203), channel_id=1, source_target_pairs={{0,8},{8,0},{16,24},{24,16},{1,9},{9,1},{17,25},{25,17},{2,10},{10... | collective-permute-start | bytes 786440 | tf_op jit(solution)/shard_map/ppermute | solution.py:23
  216.2 18.2 %collective-permute-start.42 = (bf16[64,2048]{1,0:T(8,128)(2,1)S(1)}, bf16[64,2048]{1,0:T(8,128)(2,1)S(1)}, u32[]{:S(2)}, u32[]{:S(2)}) collective-permute-start(bf16[64,2048]{1,0:T(8,128)(2,1)S(1)} %slice.207), channel_id=1, source_target_pairs={{0,8},{8,0},{16,24},{24,16},{1,9},{9,1},{17,25},{25,17},{2,10},{10... | collective-permute-start | bytes 786440 | tf_op jit(solution)/shard_map/ppermute | solution.py:23
  216.4 51.4 %collective-permute-start.23 = (bf16[64,2048]{1,0:T(8,128)(2,1)}, bf16[64,2048]{1,0:T(8,128)(2,1)S(1)}, u32[]{:S(2)}, u32[]{:S(2)}) collective-permute-start(bf16[64,2048]{1,0:T(8,128)(2,1)} %get-tuple-element.37), channel_id=1, source_target_pairs={{0,16},{8,24},{16,0},{24,8},{1,17},{9,25},{17,1},{25,9},{2,18},{10... | collective-permute-start | bytes 786440 | tf_op jit(solution)/shard_map/ppermute | solution.py:27
  232.8 36.7 %collective-permute-start.25 = (bf16[64,2048]{1,0:T(8,128)(2,1)S(1)}, bf16[64,2048]{1,0:T(8,128)(2,1)S(1)}, u32[]{:S(2)}, u32[]{:S(2)}) collective-permute-start(bf16[64,2048]{1,0:T(8,128)(2,1)S(1)} %copy-done.28), channel_id=1, source_target_pairs={{0,8},{8,0},{16,24},{24,16},{1,9},{9,1},{17,25},{25,17},{2,10},{10... | collective-permute-start | bytes 786440 | tf_op jit(solution)/shard_map/ppermute | solution.py:23
  234.3 36.6 %collective-permute-start.34 = (bf16[64,2048]{1,0:T(8,128)(2,1)}, bf16[64,2048]{1,0:T(8,128)(2,1)S(1)}, u32[]{:S(2)}, u32[]{:S(2)}) collective-permute-start(bf16[64,2048]{1,0:T(8,128)(2,1)} %get-tuple-element.44), channel_id=1, source_target_pairs={{0,16},{8,24},{16,0},{24,8},{1,17},{9,25},{17,1},{25,9},{2,18},{10... | collective-permute-start | bytes 786440 | tf_op jit(solution)/shard_map/ppermute | solution.py:27
  250.9 20.3 %collective-permute-start.36 = (bf16[64,2048]{1,0:T(8,128)(2,1)S(1)}, bf16[64,2048]{1,0:T(8,128)(2,1)S(1)}, u32[]{:S(2)}, u32[]{:S(2)}) collective-permute-start(bf16[64,2048]{1,0:T(8,128)(2,1)S(1)} %copy-done.27), channel_id=1, source_target_pairs={{0,8},{8,0},{16,24},{24,16},{1,9},{9,1},{17,25},{25,17},{2,10},{10... | collective-permute-start | bytes 786440 | tf_op jit(solution)/shard_map/ppermute | solution.py:23
  251.1 22.2 %collective-permute-start.43 = (bf16[64,2048]{1,0:T(8,128)(2,1)}, bf16[64,2048]{1,0:T(8,128)(2,1)S(1)}, u32[]{:S(2)}, u32[]{:S(2)}) collective-permute-start(bf16[64,2048]{1,0:T(8,128)(2,1)} %get-tuple-element.49), channel_id=1, source_target_pairs={{0,16},{8,24},{16,0},{24,8},{1,17},{9,25},{17,1},{25,9},{2,18},{10... | collective-permute-start | bytes 786440 | tf_op jit(solution)/shard_map/ppermute | solution.py:27
  271.2 22.8 %collective-permute-start.24 = (bf16[128,2048]{1,0:T(8,128)(2,1)S(1)}, bf16[128,2048]{1,0:T(8,128)(2,1)S(1)}, u32[]{:S(2)}, u32[]{:S(2)}) collective-permute-start(bf16[128,2048]{1,0:T(8,128)(2,1)S(1)} %pad_maximum_fusion.2), channel_id=1, source_target_pairs={{0,8},{8,0},{16,24},{24,16},{1,9},{9,1},{17,25},{25,17},{2,10},{10... | collective-permute-start | bytes 1572872 | tf_op jit(solution)/shard_map/ppermute | solution.py:23
  273.3 21.6 %collective-permute-start.26 = (bf16[128,2048]{1,0:T(8,128)(2,1)S(1)}, bf16[128,2048]{1,0:T(8,128)(2,1)S(1)}, u32[]{:S(2)}, u32[]{:S(2)}) collective-permute-start(bf16[128,2048]{1,0:T(8,128)(2,1)S(1)} %pad_maximum_fusion.3), channel_id=1, source_target_pairs={{0,16},{8,24},{16,0},{24,8},{1,17},{9,25},{17,1},{25,9},{2,18},{10... | collective-permute-start | bytes 1572872 | tf_op jit(solution)/shard_map/ppermute | solution.py:27
  277.1 28.1 %collective-permute-start.35 = (bf16[128,2048]{1,0:T(8,128)(2,1)S(1)}, bf16[128,2048]{1,0:T(8,128)(2,1)S(1)}, u32[]{:S(2)}, u32[]{:S(2)}) collective-permute-start(bf16[128,2048]{1,0:T(8,128)(2,1)S(1)} %pad_maximum_fusion.4), channel_id=1, source_target_pairs={{0,8},{8,0},{16,24},{24,16},{1,9},{9,1},{17,25},{25,17},{2,10},{10... | collective-permute-start | bytes 1572872 | tf_op jit(solution)/shard_map/ppermute | solution.py:23
  279.0 27.1 %collective-permute-start.37 = (bf16[128,2048]{1,0:T(8,128)(2,1)S(1)}, bf16[128,2048]{1,0:T(8,128)(2,1)S(1)}, u32[]{:S(2)}, u32[]{:S(2)}) collective-permute-start(bf16[128,2048]{1,0:T(8,128)(2,1)S(1)} %pad_maximum_fusion.5), channel_id=1, source_target_pairs={{0,16},{8,24},{16,0},{24,8},{1,17},{9,25},{17,1},{25,9},{2,18},{10... | collective-permute-start | bytes 1572872 | tf_op jit(solution)/shard_map/ppermute | solution.py:27
  282.8 31.6 %collective-permute-start.44 = (bf16[128,2048]{1,0:T(8,128)(2,1)S(1)}, bf16[128,2048]{1,0:T(8,128)(2,1)S(1)}, u32[]{:S(2)}, u32[]{:S(2)}) collective-permute-start(bf16[128,2048]{1,0:T(8,128)(2,1)S(1)} %pad_maximum_fusion.6), channel_id=1, source_target_pairs={{0,8},{8,0},{16,24},{24,16},{1,9},{9,1},{17,25},{25,17},{2,10},{10... | collective-permute-start | bytes 1572872 | tf_op jit(solution)/shard_map/ppermute | solution.py:23
  294.0 20.4 %collective-permute-start.46 = (bf16[128,2048]{1,0:T(8,128)(2,1)S(1)}, bf16[128,2048]{1,0:T(8,128)(2,1)S(1)}, u32[]{:S(2)}, u32[]{:S(2)}) collective-permute-start(bf16[128,2048]{1,0:T(8,128)(2,1)S(1)} %pad_maximum_fusion.7), channel_id=1, source_target_pairs={{0,16},{8,24},{16,0},{24,8},{1,17},{9,25},{17,1},{25,9},{2,18},{10... | collective-permute-start | bytes 1572872 | tf_op jit(solution)/shard_map/ppermute | solution.py:27
  294.9 25.1 %collective-permute-start.53 = (bf16[128,2048]{1,0:T(8,128)(2,1)S(1)}, bf16[128,2048]{1,0:T(8,128)(2,1)S(1)}, u32[]{:S(2)}, u32[]{:S(2)}) collective-permute-start(bf16[128,2048]{1,0:T(8,128)(2,1)S(1)} %pad_maximum_fusion.8), channel_id=1, source_target_pairs={{0,8},{8,0},{16,24},{24,16},{1,9},{9,1},{17,25},{25,17},{2,10},{10... | collective-permute-start | bytes 1572872 | tf_op jit(solution)/shard_map/ppermute | solution.py:23
  314.4 20.3 %collective-permute-start.38 = (bf16[128,2048]{1,0:T(8,128)(2,1)S(1)}, bf16[128,2048]{1,0:T(8,128)(2,1)S(1)}, u32[]{:S(2)}, u32[]{:S(2)}) collective-permute-start(bf16[128,2048]{1,0:T(8,128)(2,1)S(1)} %add_convert_fusion.2), channel_id=1, source_target_pairs={{0,4},{1,5},{2,6},{3,7},{4,0},{5,1},{6,2},{7,3},{8,12},{9,13},{10,... | collective-permute-start | bytes 1572872 | tf_op jit(solution)/shard_map/ppermute | solution.py:36
  314.6 20.1 %collective-permute-start.47 = (bf16[128,2048]{1,0:T(8,128)(2,1)S(1)}, bf16[128,2048]{1,0:T(8,128)(2,1)S(1)}, u32[]{:S(2)}, u32[]{:S(2)}) collective-permute-start(bf16[128,2048]{1,0:T(8,128)(2,1)S(1)} %add_convert_fusion.1), channel_id=1, source_target_pairs={{0,6},{1,7},{2,0},{3,1},{4,2},{5,3},{6,4},{7,5},{8,14},{9,15},{10,... | collective-permute-start | bytes 1572872 | tf_op jit(solution)/shard_map/ppermute | solution.py:36
  (53 other events, 700.8 us)

commit v2 on v1

v2 whole, which is shorter than its diff:
```python
import functools
import math

import jax
import jax.numpy as jnp
from jax import lax
from jax.experimental import pallas as pl
from jax.experimental.pallas import tpu as pltpu
from jax.sharding import PartitionSpec as P

HEAD_SIZE = 128
KEY_BLOCK = 512
SPLIT = 8
FF_TILE = 256
VMEM_BYTES = 56 * 1024 * 1024
LOW = -1e30


def after(value, *others):
    return lax.optimization_barrier((value, *others))[0]


def swap_x(value):
    return lax.ppermute(value, "grp", [(i, i ^ 1) for i in range(lax.axis_size("grp"))])


def swap_y(value):
    return lax.ppermute(value, "grp", [(i, i ^ 2) for i in range(lax.axis_size("grp"))])


def swap_core(value):
    return lax.ppermute(value, "dev", [(i, i ^ 1) for i in range(lax.axis_size("dev"))])


def turn(value, planes):
    count = lax.axis_size("dev")
    return lax.ppermute(value, "dev", [(i, (i - 2 * planes) % count) for i in range(count)])


def earlier(value, steps, sources=lambda source: True):
    count = lax.axis_size("dev")
    pairs = [(i, i + steps) for i in range(count - steps) if sources(i)]
    return lax.ppermute(value, "dev", pairs)


def hold_kernel(*refs):
    del refs


def hold(values, *waits):
    anywhere = pl.BlockSpec(memory_space=pl.ANY)
    return pl.pallas_call(
        hold_kernel,
        in_specs=[anywhere] * (len(values) + len(waits)),
        out_specs=[anywhere] * len(values),
        out_shape=[jax.ShapeDtypeStruct(v.shape, v.dtype) for v in values],
        input_output_aliases={i: i for i in range(len(values))},
        cost_estimate=pl.CostEstimate(flops=0, bytes_accessed=0, transcendentals=0),
        name="hold",
    )(*values, *waits)


def gather_keys(keys, values, reach):
    own = jnp.concatenate([keys, values], axis=1)
    whole = reach // 2
    lanes = [own] + [earlier(own, 2 * j) for j in range(1, whole + 1)]
    pieces = [piece for lane in lanes[::-1] for piece in (lane, swap_core(lane))]
    if reach % 2:
        pieces = [earlier(own, reach, lambda source: source % 2 == 1)] + pieces
    return pieces


def attend_kernel(place, bounds, *refs, shards, waits):
    q_ref, start_ref = refs[:2]
    pieces = refs[2 : 2 + shards]
    out_ref, q_all, kv_ref, top, total = refs[2 + shards + waits :]
    size = pieces[0].shape[0]
    core = place[1]
    for i, piece in enumerate(pieces):
        lone = shards % 2
        if i < lone:
            at = 0
        else:
            pair = i - (i - lone) % 2
            at = pair + (core if pair == i else 1 - core)
        kv_ref[pl.ds(pl.multiple_of(at * size, size), size), :] = piece[...]
    rows = q_ref.shape[0]
    heads = q_ref.shape[1] // HEAD_SIZE
    for h in range(heads):
        q_all[h * rows : (h + 1) * rows, :] = q_ref[:, h * HEAD_SIZE : (h + 1) * HEAD_SIZE]
    top[...] = jnp.full_like(top, LOW)
    total[...] = jnp.zeros_like(total)
    block_index = place[0]
    q_low = bounds[0] + block_index * rows
    first_start, last_start = bounds[1 + 2 * block_index], bounds[2 + 2 * block_index]
    factor = math.log2(math.e) / math.sqrt(HEAD_SIZE)

    def step(block, masked):
        low = pl.multiple_of(block * KEY_BLOCK, KEY_BLOCK)
        key = kv_ref[pl.ds(low, KEY_BLOCK), :HEAD_SIZE]
        value = kv_ref[pl.ds(low, KEY_BLOCK), HEAD_SIZE:]
        value = jnp.concatenate([value, jnp.ones_like(value)], axis=1)
        if masked:
            key_pos = low + lax.broadcasted_iota(jnp.int32, (rows, KEY_BLOCK), 1)
            q_pos = q_low + lax.broadcasted_iota(jnp.int32, (rows, KEY_BLOCK), 0)
            seen = (key_pos >= start_ref[...]) & (key_pos <= q_pos)
        part_heads = heads // SPLIT
        size = part_heads * rows
        scores = []
        for r in range(SPLIT):
            scores.append(lax.dot_general(
                q_all[r * size : (r + 1) * size, :], key, (((1,), (1,)), ((), ())), preferred_element_type=jnp.float32
            ))
        for r in range(SPLIT):
            span = slice(r * size, (r + 1) * size)
            score = scores[r] * factor
            if masked:
                score = jnp.where(seen[None], score.reshape(part_heads, rows, KEY_BLOCK), LOW)
                score = score.reshape(size, KEY_BLOCK)
            old = top[span, :]
            new = jnp.maximum(old, jnp.max(score, axis=1, keepdims=True))
            weight = jnp.exp2(score - jnp.concatenate([new] * (KEY_BLOCK // HEAD_SIZE), axis=1))
            shrink = jnp.exp2(old - new)
            added = jnp.dot(weight.astype(jnp.bfloat16), value, preferred_element_type=jnp.float32)
            total[span, :] = total[span, :] * jnp.concatenate([shrink, shrink], axis=1) + added
            top[span, :] = new

    def loop(low, high, masked):
        def body(block, carry):
            step(block, masked)
            return carry

        lax.fori_loop(low, high, body, 0)

    begin = first_start // KEY_BLOCK
    end = (q_low + rows - 1) // KEY_BLOCK + 1
    inner_low = jnp.minimum((last_start + KEY_BLOCK - 1) // KEY_BLOCK, end)
    inner_high = jnp.maximum((q_low + 1) // KEY_BLOCK, inner_low)
    loop(begin, inner_low, True)
    loop(inner_low, inner_high, False)
    loop(inner_high, end, True)
    for h in range(heads):
        part = total[h * rows : (h + 1) * rows, :]
        out_ref[:, h * HEAD_SIZE : (h + 1) * HEAD_SIZE] = (
            part[:, :HEAD_SIZE] / part[:, HEAD_SIZE:]
        ).astype(out_ref.dtype)


def attend(block, queries, pieces, starts, bounds, rows, waits=()):
    width = queries.shape[1]
    heads = width // HEAD_SIZE
    length = len(pieces) * pieces[0].shape[0]
    pairs = heads * rows * length // 2
    place = jnp.stack([block, lax.axis_index("dev") % 2]).astype(jnp.int32)
    return pl.pallas_call(
        functools.partial(attend_kernel, shards=len(pieces), waits=len(waits)),
        grid_spec=pltpu.PrefetchScalarGridSpec(
            num_scalar_prefetch=2,
            grid=(1,),
            in_specs=[
                pl.BlockSpec((rows, width), lambda i, place, bounds: (place[0], 0)),
                pl.BlockSpec((rows, 1), lambda i, place, bounds: (place[0], 0)),
            ]
            + [pl.BlockSpec(p.shape, lambda i, place, bounds: (0, 0)) for p in pieces]
            + [pl.BlockSpec(memory_space=pl.ANY)] * len(waits),
            out_specs=pl.BlockSpec((rows, width), lambda i, place, bounds: (0, 0)),
            scratch_shapes=[
                pltpu.VMEM((heads * rows, HEAD_SIZE), jnp.bfloat16),
                pltpu.VMEM((length, 2 * HEAD_SIZE), jnp.bfloat16),
                pltpu.VMEM((heads * rows, HEAD_SIZE), jnp.float32),
                pltpu.VMEM((heads * rows, 2 * HEAD_SIZE), jnp.float32),
            ],
        ),
        out_shape=jax.ShapeDtypeStruct((rows, width), jnp.bfloat16),
        compiler_params=pltpu.CompilerParams(vmem_limit_bytes=VMEM_BYTES),
        cost_estimate=pl.CostEstimate(
            flops=4 * pairs * HEAD_SIZE, bytes_accessed=4 * length * HEAD_SIZE, transcendentals=pairs
        ),
        name="attend",
    )(place, bounds, queries, starts[:, None], *pieces, *waits)


def feed_kernel(*refs, blocks, first, waits):
    step = pl.program_id(0)
    last = pl.num_programs(0) - 1
    refs = list(refs)
    incoming = [refs.pop(0) for _ in range(5 * blocks)] if first else None
    slot_of, gates, gate_ref, up_ref, down_ref = (refs.pop(0) for _ in range(5))
    if not first:
        taken, earlier_given = refs.pop(0), refs.pop(0)
    refs = refs[waits:]
    if first:
        given, other, taken, summed = refs
    else:
        outgoing, (given, summed) = refs[: 5 * blocks], refs[5 * blocks :]
    tokens = slot_of.shape[3]
    half = tokens // 2
    slots = given.shape[0] // (2 * blocks)
    each = slots // 2

    def chosen(p, e, b):
        at = 2 * p + b
        mine = slot_of[at // 4, e, at % 4 : at % 4 + 1, :]
        return lax.broadcasted_iota(jnp.int32, (each, tokens), 0) == mine

    def pick(p):
        lines = []
        for e in range(2):
            for b in range(2):
                found = chosen(p, e, b).astype(jnp.float32)
                zeros = jnp.zeros_like(found)
                lines.append(jnp.concatenate([zeros, found] if b else [found, zeros], axis=1))
        return jnp.concatenate(lines).astype(jnp.bfloat16)

    def share(e):
        parts = []
        for p in range(2 * blocks):
            for b in range(2):
                at = 2 * p + b
                gate = gates[at // 4, e, at % 4 : at % 4 + 1, :]
                parts.append(jnp.sum(jnp.where(chosen(p, e, b), gate, 0.0), axis=1, keepdims=True))
        return jnp.concatenate(parts)

    if first:

        @pl.when(step == 0)
        def _():
            for p in range(2 * blocks):
                at = 5 * (p // 2) + 2 * (p % 2)
                pieces = incoming[at : at + 2 + p % 2]
                held = jnp.concatenate([piece[...] for piece in pieces])
                found = jnp.dot(pick(p), held, preferred_element_type=jnp.float32)
                found = found.astype(taken.dtype)
                taken[p * slots : (p + 1) * slots, :] = found[:slots]
                other[p * slots : (p + 1) * slots, :] = found[slots:]

    rows = taken[...]
    gate = jnp.dot(rows, gate_ref[...], preferred_element_type=jnp.float32)
    up = jnp.dot(rows, up_ref[...], preferred_element_type=jnp.float32)
    hidden = (gate / (1.0 + jnp.exp(-gate)) * up).astype(jnp.bfloat16)
    part = jnp.dot(hidden, down_ref[...], preferred_element_type=jnp.float32)

    @pl.when(step == 0)
    def _():
        summed[...] = part

    @pl.when(step > 0)
    def _():
        summed[...] += part

    @pl.when(step == last)
    def _():
        given[...] = (summed[...] * share(0 if first else 1)).astype(given.dtype)
        if first:
            return
        for p in range(2 * blocks):
            at = 5 * (p // 2) + 2 * (p % 2)
            place = slice(p * slots, (p + 1) * slots)
            rows = jnp.concatenate([earlier_given[place, :], given[place, :]])
            back = lax.dot_general(
                pick(p), rows, (((0,), (0,)), ((), ())), preferred_element_type=jnp.float32
            ).astype(jnp.bfloat16)
            outgoing[at][...] = back[:tokens]
            if p % 2 == 0:
                outgoing[at + 1][...] = back[tokens:]
            else:
                outgoing[at + 1][...] = back[tokens : tokens + half]
                outgoing[at + 2][...] = back[tokens + half :]


def feed(first, inputs, slot_of, gates, slots, weights, extra, rows, waits=()):
    width, ff = weights[0].shape
    tile = math.gcd(ff, FF_TILE)
    blocks = slot_of.shape[0]
    slots = 4 * blocks * slots

    def whole(shape):
        return pl.BlockSpec(shape, lambda i: (0,) * len(shape))

    shapes = ([(rows, width)] * 3 + [(rows // 2, width), (rows - rows // 2, width)]) * blocks
    operands = [*inputs, slot_of, gates, *weights, *extra]
    specs = [whole(v.shape) for v in operands]
    at = len(inputs) + 2
    specs[at : at + 3] = [
        pl.BlockSpec((width, tile), lambda i: (0, i)),
        pl.BlockSpec((width, tile), lambda i: (0, i)),
        pl.BlockSpec((tile, width), lambda i: (i, 0)),
    ]
    specs += [pl.BlockSpec(memory_space=pl.ANY)] * len(waits)
    results = [(slots, width)] * 2 if first else shapes
    kept = pltpu.VMEM((slots, width), jnp.bfloat16)
    return pl.pallas_call(
        functools.partial(feed_kernel, blocks=blocks, first=first, waits=len(waits)),
        grid=(ff // tile,),
        in_specs=specs,
        out_specs=[whole(s) for s in results],
        out_shape=[jax.ShapeDtypeStruct(s, jnp.bfloat16) for s in results],
        scratch_shapes=[kept, pltpu.VMEM((slots, width), jnp.float32)],
        compiler_params=pltpu.CompilerParams(vmem_limit_bytes=VMEM_BYTES),
        cost_estimate=pl.CostEstimate(
            flops=6 * slots * width * ff,
            bytes_accessed=6 * width * ff + 12 * blocks * rows * width,
            transcendentals=slots * ff,
        ),
        name="feed_first" if first else "feed_second",
    )(*operands, *waits)


def collect_near(own, by_x, by_y, from_a, from_b, *waits):
    half = from_a.shape[0]
    if waits:
        by_x, by_y = hold([by_x, by_y], *waits)
    by_y = jnp.concatenate([by_y[:half] + from_a, by_y[half:]])
    by_x = jnp.concatenate([by_x[:half], by_x[half:] + from_b])
    return own, swap_x(by_x), swap_y(by_y)


def add_up(parts):
    return sum(part.astype(jnp.float32) for part in parts)


def routing(ids, gates, expert_count, waits):
    dev_size = lax.axis_size("dev")
    planes = dev_size // 2
    named = ids.T[None] == jnp.arange(expert_count, dtype=jnp.int32)[:, None, None]
    [dense] = hold([jnp.sum(jnp.where(named, gates.T[None], 0.0), axis=1)], *waits)
    pair = jnp.stack([dense, swap_x(dense)])
    four = jnp.concatenate([pair, swap_y(pair)])
    every = jnp.stack([four] + [turn(four, k) for k in range(1, planes)])
    me = lax.axis_index("grp") * dev_size + lax.axis_index("dev")
    mine = jnp.stack(
        [lax.dynamic_index_in_dim(every, e, 2, keepdims=False) for e in (me, me ^ 1)], axis=1
    )
    named = mine > 0
    tokens = mine.shape[-1]
    before = jnp.triu(jnp.ones((tokens, tokens), jnp.bfloat16), 1)
    rank = jnp.dot(named.astype(jnp.bfloat16), before, preferred_element_type=jnp.float32)
    return jnp.where(named, rank, -1.0).astype(jnp.int32), mine, (pair, four)


def shards(
    queries,
    keys,
    values,
    doc_ids,
    out_weight,
    norm_gain,
    expert_ids,
    gate_values,
    expert_gate,
    expert_up,
    expert_down,
):
    own_rows = queries.shape[0]
    grp_size = lax.axis_size("grp")
    dev_size = lax.axis_size("dev")
    planes = dev_size // 2
    group, device = lax.axis_index("grp"), lax.axis_index("dev")
    dev_rows = own_rows // grp_size
    width = out_weight.shape[1]
    top_count = expert_ids.shape[2]
    expert_count = grp_size * dev_size
    capacity = max(2, 3 * dev_rows * top_count // (2 * expert_count))
    slots = -(-capacity // 16) * 16
    doc_reach = dev_size * own_rows // 2 + own_rows
    reach = min(dev_size - 1, (doc_reach + own_rows - 1) // own_rows)

    pieces = gather_keys(keys, values, reach)
    own_low = (len(pieces) - 2 + device % 2) * own_rows
    own_docs = lax.dynamic_slice_in_dim(doc_ids, device * own_rows, own_rows, 0)
    starts = jnp.sum((doc_ids[None, :] < own_docs[:, None]).astype(jnp.int32), axis=1)
    starts = starts - device * own_rows + own_low
    ends = jnp.stack([starts[::dev_rows], starts[dev_rows - 1 :: dev_rows]], axis=1)
    bounds = jnp.concatenate([own_low[None], ends.reshape(-1)]).astype(jnp.int32)

    slot_of, gates, steps = routing(expert_ids[0], gate_values[0], expert_count, pieces[-2:])
    own_weights = [expert_gate[0], expert_up[0], expert_down[0]]
    other_weights = [swap_core(w) for w in own_weights]

    def part(block, *waits):
        attended = attend(block, queries, pieces, starts, bounds, dev_rows, waits)
        return jnp.dot(attended, out_weight, preferred_element_type=jnp.float32)

    half = dev_rows // 2
    far = part(group ^ 3).astype(jnp.bfloat16)
    from_a, from_b = swap_x(far[:half]), swap_y(far[half:])
    by_x = part(group ^ 1, far, steps[0], *other_weights).astype(jnp.bfloat16)
    by_y = part(group ^ 2, by_x, steps[1]).astype(jnp.bfloat16)
    own = part(group, slot_of, gates, from_a, from_b)
    projected = add_up(collect_near(own, by_x, by_y, from_a, from_b))
    normed = (
        projected
        * lax.rsqrt(jnp.mean(projected * projected, axis=-1, keepdims=True) + 1e-06)
        * norm_gain
    ).astype(jnp.bfloat16)

    order = list(range(planes))
    turned = order[1:] + order[:1]
    sets = [turned[i : i + 2] for i in range(0, planes, 2)]
    blocks, done = {}, {}

    def feed_first(members, *waits):
        routes = [jnp.stack([part[k] for k in members]) for part in (slot_of, gates)]
        inputs = [b for k in members for b in blocks[k]]
        results = feed(True, inputs, *routes, slots, own_weights, [], dev_rows, waits)
        return members, routes, *results

    def feed_second(state, *waits):
        members, routes, given, other = state
        out = feed(False, [], *routes, slots, other_weights, [other, given], dev_rows, waits)
        for i, k in enumerate(members):
            done[k] = out[5 * i : 5 * i + 5]
        return out[0]

    def relay(near, *waits):
        first, second = halves(*near, *waits) if waits else (near[0][:half], near[1][half:])
        return swap_y(first), swap_x(second)

    near, sent, fars = (), [], [(), ()]

    def launch(k):
        nonlocal near
        block = normed
        if k:
            block = jnp.copy(normed)
            if len(sent) > 1:
                [block] = hold([block], *sent[-2])
            [block] = hold([turn(block, k)], *near, *fars[-2])
        near = swap_x(block), swap_y(block)
        blocks[k] = [block]

    def relay(k, *waits):
        nonlocal near
        near = hold(near, *waits) if waits else near
        sent.append((near[0][:half], near[1][half:]))
        far = swap_y(sent[-1][0]), swap_x(sent[-1][1])
        fars.append(far)
        blocks[k] += [*near, *far]
        return far

    launch(0)
    far = relay(0)
    for i, members in enumerate(sets[:-1]):
        for k in members:
            if k not in blocks:
                launch(k)
                relay(k)
        following = next(k for k in sets[i + 1] if k)
        state = feed_first(members)
        launch(following)
        far = relay(following, state[2])
        feed_second(state, *near)

    early = [k for members in sets[:-1][::-1] for k in members[::-1]]
    late = [k for k in sets[-1] if k] + [0]
    froms, sums = {}, []

    def far_part(k):
        froms[k] = swap_x(done[k][3]), swap_y(done[k][4])
        return froms[k]

    def near_part(k, *waits):
        parts = collect_near(*done[k][:3], *froms[k], *waits)
        summed = add_up(parts)
        if k:
            summed = turn(summed.astype(jnp.bfloat16), planes - k).astype(jnp.float32)
        sums.append(summed)
        return parts[1:]

    def held(k, *waits):
        done[k] = [*done[k][:3], *hold(done[k][3:5], *waits)]

    chain = far
    for k in early[:1]:
        held(k, *chain)
        chain = far_part(k)
    state = feed_first(sets[-1], *chain)
    arrived = ()
    for k in early[:1]:
        arrived = near_part(k)
    for k in early[1:]:
        held(k, *chain)
        chain = far_part(k)
    feed_second(state, *arrived, *chain)
    for k in early[1:]:
        arrived = near_part(k, state[2])
    chain = arrived
    for k in late:
        held(k, *chain)
        chain = far_part(k)
        near_part(k)
    return (projected + sum(sums)).astype(jnp.bfloat16)[None]


def solution(mesh):
    return jax.shard_map(
        shards,
        mesh=mesh,
        in_specs=(
            P("dev", "grp"),
            P("dev", "grp"),
            P("dev", "grp"),
            P(),
            P("grp", None),
            P(),
            P("dev", "grp", None),
            P("dev", "grp", None),
            P(("grp", "dev"), None, None),
            P(("grp", "dev"), None, None),
            P(("grp", "dev"), None, None),
        ),
        out_specs=P("dev", "grp", None),
        check_vma=False,
    )
```

time: 339 us -> 288 us (0.85)
  waiting for transfers between devices: 131 us -> 77.9 us
  other arithmetic: 16.3 us -> 29.8 us
  Pallas kernels: 77 us -> 65 us
    ppermute x9, waiting for transfers between devices: 33.4 us -> 7.34 us  [turn(): lax.ppermute(value, 'dev', [(i, (i - 2 * planes) % count) for i in range(...]
    ppermute x19, waiting for transfers between devices: 52.6 us -> 38.5 us  [swap_x(): lax.ppermute(value, 'grp', [(i, i ^ 1) for i in range(lax.axis_size('grp'...]
    pallas_call x8 -> x20, Pallas kernels: 77 us -> 65 us  [the longest x4 47.9 us: feed(): pl.pallas_call(functools.partial(feed_kernel, blocks=blocks, first=first,...]
    ppermute x19, waiting for transfers between devices: 43.4 us -> 32.1 us  [swap_y(): lax.ppermute(value, 'grp', [(i, i ^ 2) for i in range(lax.axis_size('grp'...]
    ppermute x9, starting transfers between devices: 24.2 us -> 15.7 us  [turn(): lax.ppermute(value, 'dev', [(i, (i - 2 * planes) % count) for i in range(...]
    unnamed x60 -> x87, local copies, waits for them, and re-layouts: 2.27 us -> 9.2 us
    ppermute x6, starting transfers between devices: 4.13 us -> 10.1 us  [swap_core(): lax.ppermute(value, 'dev', [(i, i ^ 1) for i in range(lax.axis_size('dev'...]
    convert_element_type x5 -> x3, other arithmetic: 0.93 us -> 6.15 us  [near_part(): summed = turn(summed.astype(jnp.bfloat16), planes - k).astype(jnp.float32)]
  transfers between devices with their start and end apart: 56 -> 56, of which waited for: 23 -> 20; matrix products, arithmetic and copies ran while one was open for 10% -> 18% of each run, Pallas kernels for 22% -> 23%
where the time goes in v2:
time: 288 us; the launch traced here: 286 us
  starting transfers between devices  80.7 us (28%)
  waiting for transfers between devices  77.9 us (27%)
  Pallas kernels  65 us (23%)
  other arithmetic  29.8 us (10%)
  local copies, waits for them, and re-layouts  22.7 us (8%)
  matrix products  8.99 us (3%)
    pallas_call x4, Pallas kernels, feed(): pl.pallas_call(functools.partial(feed_kernel, blocks=blocks, first=first,...  47.9 us
    ppermute x19, waiting for transfers between devices, swap_x(): lax.ppermute(value, 'grp', [(i, i ^ 1) for i in range(lax.axis_size('grp'...  38.5 us
    ppermute x19, waiting for transfers between devices, swap_y(): lax.ppermute(value, 'grp', [(i, i ^ 2) for i in range(lax.axis_size('grp'...  32.1 us
    ppermute x19, starting transfers between devices, swap_x(): lax.ppermute(value, 'grp', [(i, i ^ 1) for i in range(lax.axis_size('grp'...  22 us
    ppermute x19, starting transfers between devices, swap_y(): lax.ppermute(value, 'grp', [(i, i ^ 2) for i in range(lax.axis_size('grp'...  21.4 us
    pallas_call x4, Pallas kernels, attend(): pl.pallas_call(functools.partial(attend_kernel, shards=len(pieces), waits...  17.1 us
    ppermute x9, starting transfers between devices, turn(): lax.ppermute(value, 'dev', [(i, (i - 2 * planes) % count) for i in range(...  15.7 us
    ppermute x3, starting transfers between devices, earlier(): return lax.ppermute(value, 'dev', pairs)  11.5 us
  transfers between devices with their start and end apart: 56, of which 20 were waited for; matrix products, arithmetic and copies ran while one was open for 18% of the time, Pallas kernels for 23%

profile of v2, /device:TPU:0, one launch (start us, length us, event | category | flops | bytes accessed | tf_op | source)
XLA Modules:
  0.0 285.6 jit_solution(1305527421030900066)
XLA Ops:
  4.2 6.6 %collective-permute-start.1 = (bf16[512,256]{1,0:T(8,128)(2,1)}, bf16[512,256]{1,0:T(8,128)(2,1)}, u32[]{:S(2)}, u32[]{:S(2)}) collective-permute-start(bf16[512,256]{1,0:T(8,128)(2,1)} %constant_dynamic-update-slice_fusion.refs_1_.refs_7_), channel_id=1, source_target_pairs={{0,4},{1,5},{2,6},{3,7},{8,12},{9,13},{10,14},{11,15},{16,20},{17,... | collective-permute-start | bytes 786440 | tf_op jit(solution)/shard_map/ppermute | solution.py:43
  14.8 4.2 %collective-permute-start.3 = (bf16[512,256]{1,0:T(8,128)(2,1)}, bf16[512,256]{1,0:T(8,128)(2,1)}, u32[]{:S(2)}, u32[]{:S(2)}) collective-permute-start(bf16[512,256]{1,0:T(8,128)(2,1)} %constant_dynamic-update-slice_fusion.refs_1_.refs_7_), channel_id=1, source_target_pairs={{0,2},{1,3},{2,4},{3,5},{4,6},{5,7},{8,10},{9,11},{10,12},{11,13},... | collective-permute-start | bytes 786440 | tf_op jit(solution)/shard_map/ppermute | solution.py:43
  21.1 1.9 collective-permute-done.6
  27.2 8.6 %collective-permute-start.2 = (bf16[512,256]{1,0:T(8,128)(2,1)}, bf16[512,256]{1,0:T(8,128)(2,1)}, u32[]{:S(2)}, u32[]{:S(2)}) collective-permute-start(bf16[512,256]{1,0:T(8,128)(2,1)} %collective-permute-done.1.refs_3_), channel_id=1, source_target_pairs={{0,1},{1,0},{2,3},{3,2},{4,5},{5,4},{6,7},{7,6},{8,9},{9,8},{10,11... | collective-permute-start | bytes 786440 | tf_op jit(solution)/shard_map/ppermute | solution.py:32
  39.4 4.1 %collective-permute-start.8 = (f32[4,32,128]{2,1,0:T(8,128)S(1)}, f32[4,32,128]{2,1,0:T(8,128)}, u32[]{:S(2)}, u32[]{:S(2)}) collective-permute-start(f32[4,32,128]{2,1,0:T(8,128)S(1)} %get-tuple-element.102.refs_10_), channel_id=1, source_target_pairs={{0,6},{1,7},{2,0},{3,1},{4,2},{5,3},{6,4},{7,5},{8,14},{9,15},{10,... | collective-permute-start | bytes 196616 | tf_op jit(solution)/shard_map/ppermute | solution.py:37
  43.5 4.2 %attend.4 = bf16[128,1024]{1,0:T(8,128)(2,1)} custom-call(s32[2]{0:T(128)} %pad_add_fusion.4.place, s32[9]{0:T(128)} %pad_add_fusion.3.bounds, bf16[512,1024]{1,0:T(8,128)(2,1)} %refs_0_.7, s32[512,1]{1,0:T(8,128)} %copy.38.refs_1_, bf16[512,256]{1,0:T(8,128)(2,1)} %copy-done.14, bf16[512,256]{1,0:T(8,128)(2,1)} %collective-permute-done.1.refs_3_, ...), custom_call_target="tpu_custom_call" | custom-call | flops 939524096 | bytes 1835008 | tf_op jit(solution)/shard_map/attend/pallas_call | solution.py:155
  47.8 3.0 %convolution_convert_fusion.2.refs_9_ = bf16[128,2048]{1,0:T(8,128)(2,1)S(1)} fusion(bf16[128,1024]{1,0:T(8,128)(2,1)} %attend.4, bf16[1024,2048]{1,0:T(8,128)(2,1)} %param.15), kind=kOutput, calls=%fused_computation.5 | convolution fusion | flops 537133056 | bytes 4980736 | tf_op jit(solution)/shard_map/dot_general | solution.py:382
  51.7 2.5 collective-permute-start.10
  57.3 4.2 %attend.6 = bf16[128,1024]{1,0:T(8,128)(2,1)} custom-call(s32[2]{0:T(128)} %pad_add_fusion.5.place, s32[9]{0:T(128)} %pad_add_fusion.3.bounds, bf16[512,1024]{1,0:T(8,128)(2,1)} %refs_0_.7, s32[512,1]{1,0:T(8,128)} %copy.38.refs_1_, bf16[512,256]{1,0:T(8,128)(2,1)} %copy-done.14, bf16[512,256]{1,0:T(8,128)(2,1)} %collective-permute-done.1.refs_3_, ...), custom_call_target="tpu_custom_call" | custom-call | flops 939524096 | bytes 1835008 | tf_op jit(solution)/shard_map/attend/pallas_call | solution.py:155
  66.1 4.4 %attend.7 = bf16[128,1024]{1,0:T(8,128)(2,1)} custom-call(s32[2]{0:T(128)} %pad_add_fusion.6.place, s32[9]{0:T(128)} %pad_add_fusion.3.bounds, bf16[512,1024]{1,0:T(8,128)(2,1)} %refs_0_.7, s32[512,1]{1,0:T(8,128)} %copy.38.refs_1_, bf16[512,256]{1,0:T(8,128)(2,1)} %copy-done.14, bf16[512,256]{1,0:T(8,128)(2,1)} %collective-permute-done.1.refs_3_, ...), custom_call_target="tpu_custom_call" | custom-call | flops 939524096 | bytes 1835008 | tf_op jit(solution)/shard_map/attend/pallas_call | solution.py:155
  76.2 4.2 %attend.5 = bf16[128,1024]{1,0:T(8,128)(2,1)} custom-call(s32[2]{0:T(128)} %pad_add_fusion.2.place, s32[9]{0:T(128)} %pad_add_fusion.3.bounds, bf16[512,1024]{1,0:T(8,128)(2,1)} %refs_0_.7, s32[512,1]{1,0:T(8,128)} %copy.38.refs_1_, bf16[512,256]{1,0:T(8,128)(2,1)} %copy-done.14, bf16[512,256]{1,0:T(8,128)(2,1)} %collective-permute-done.1.refs_3_, ...), custom_call_target="tpu_custom_call" | custom-call | flops 939524096 | bytes 1835008 | tf_op jit(solution)/shard_map/attend/pallas_call | solution.py:155
  80.5 6.3 %collective-permute-done.17 = bf16[128,2048]{1,0:T(8,128)(2,1)S(1)} collective-permute-done((bf16[128,2048]{1,0:T(8,128)(2,1)S(1)}, bf16[128,2048]{1,0:T(8,128)(2,1)S(1)}, u32[]{:S(2)}, u32[]{:S(2)}) %collective-permute-start.17) | collective-permute-done | bytes 524320 | tf_op jit(solution)/shard_map/ppermute | solution.py:28
  86.8 1.9 multiply_reduce_fusion
  92.7 10.0 %collective-permute-done.19.refs_1_.refs_6_ = bf16[128,2048]{1,0:T(8,128)(2,1)S(1)} collective-permute-done((bf16[128,2048]{1,0:T(8,128)(2,1)S(1)}, bf16[128,2048]{1,0:T(8,128)(2,1)S(1)}, u32[]{:S(2)}, u32[]{:S(2)}) %collective-permute-start.19) | collective-permute-done | bytes 524320 | tf_op jit(solution)/shard_map/ppermute | solution.py:24
  104.6 6.4 %collective-permute-start.25 = (bf16[128,2048]{1,0:T(8,128)(2,1)}, bf16[128,2048]{1,0:T(8,128)(2,1)S(1)}, u32[]{:S(2)}, u32[]{:S(2)}) collective-permute-start(bf16[128,2048]{1,0:T(8,128)(2,1)} %hold.14), channel_id=1, source_target_pairs={{0,4},{1,5},{2,6},{3,7},{4,0},{5,1},{6,2},{7,3},{8,12},{9,13},{10,... | collective-permute-start | bytes 1572872 | tf_op jit(solution)/shard_map/ppermute | solution.py:37
  115.1 14.3 %collective-permute-done.26.refs_3_.refs_8_ = bf16[64,2048]{1,0:T(8,128)(2,1)S(1)} collective-permute-done((bf16[64,2048]{1,0:T(8,128)(2,1)}, bf16[64,2048]{1,0:T(8,128)(2,1)S(1)}, u32[]{:S(2)}, u32[]{:S(2)}) %collective-permute-start.26) | collective-permute-done | bytes 262176 | tf_op jit(solution)/shard_map/ppermute | solution.py:28
  129.4 4.3 %collective-permute-done.25.refs_0_ = bf16[128,2048]{1,0:T(8,128)(2,1)S(1)} collective-permute-done((bf16[128,2048]{1,0:T(8,128)(2,1)}, bf16[128,2048]{1,0:T(8,128)(2,1)S(1)}, u32[]{:S(2)}, u32[]{:S(2)}) %collective-permute-start.25) | collective-permute-done | bytes 524320 | tf_op jit(solution)/shard_map/ppermute | solution.py:37
  143.8 6.9 %collective-permute-done.28.refs_6_.refs_1_ = bf16[128,2048]{1,0:T(8,128)(2,1)S(1)} collective-permute-done((bf16[128,2048]{1,0:T(8,128)(2,1)}, bf16[128,2048]{1,0:T(8,128)(2,1)S(1)}, u32[]{:S(2)}, u32[]{:S(2)}) %collective-permute-start.28) | collective-permute-done | bytes 524320 | tf_op jit(solution)/shard_map/ppermute | solution.py:24
  163.3 11.8 %feed_first.2 = (bf16[384,2048]{1,0:T(8,128)(2,1)}, bf16[384,2048]{1,0:T(8,128)(2,1)}) custom-call(bf16[128,2048]{1,0:T(8,128)(2,1)} %hold.13.refs_0_, bf16[128,2048]{1,0:T(8,128)(2,1)} %copy-done.10, bf16[128,2048]{1,0:T(8,128)(2,1)} %copy-done.11, bf16[64,2048]{1,0:T(8,128)(2,1)} %copy-done.31, bf16[64,2048]{1,0:T(8,128)(2,1)} %copy-done.32, ...), custom_call_target="tpu_custom_call" | custom-call | flops 3623878656 | bytes 15728640 | tf_op jit(solution)/shard_map/feed_first/pallas_call | solution.py:292
  180.5 11.9 %feed_second.2 = (bf16[128,2048]{1,0:T(8,128)(2,1)}, bf16[128,2048]{1,0:T(8,128)(2,1)}, bf16[128,2048]{1,0:T(8,128)(2,1)}, bf16[64,2048]{1,0:T(8,128)(2,1)}, bf1...) custom-call(s32[2,2,4,128]{3,2,1,0:T(4,128)} %stack.111.refs_10_.ref, ...), custom_call_target="tpu_custom_call" | custom-call | flops 3623878656 | bytes 15728640 | tf_op jit(solution)/shard_map/feed_second/pallas_call | solution.py:292
  196.2 3.6 %collective-permute-done.39.refs_15_.refs_2_ = bf16[64,2048]{1,0:T(8,128)(2,1)S(1)} collective-permute-done((bf16[64,2048]{1,0:T(8,128)(2,1)}, bf16[64,2048]{1,0:T(8,128)(2,1)S(1)}, u32[]{:S(2)}, u32[]{:S(2)}) %collective-permute-start.39) | collective-permute-done | bytes 262176 | tf_op jit(solution)/shard_map/ppermute | solution.py:24
  202.3 1.8 collective-permute-done.37.refs_16_.refs_3_
  209.7 11.8 %feed_first.3 = (bf16[384,2048]{1,0:T(8,128)(2,1)}, bf16[384,2048]{1,0:T(8,128)(2,1)}) custom-call(bf16[128,2048]{1,0:T(8,128)(2,1)} %hold.17.refs_0_, bf16[128,2048]{1,0:T(8,128)(2,1)} %get-tuple-element.43.refs_7_.refs_1_, bf16[128,2048]{1,0:T(8,128)(2,1)} %get-tuple-element.44.refs_8_.refs_2_, bf16[64,2048]{1,0:T(8,128)(2,1)} %copy-done.27, ...), custom_call_target="tpu_custom_call" | custom-call | flops 3623878656 | bytes 15728640 | tf_op jit(solution)/shard_map/feed_first/pallas_call | solution.py:292
  225.5 2.5 add_convert_fusion.3
  228.0 12.3 %feed_second.3 = (bf16[128,2048]{1,0:T(8,128)(2,1)}, bf16[128,2048]{1,0:T(8,128)(2,1)}, bf16[128,2048]{1,0:T(8,128)(2,1)}, bf16[64,2048]{1,0:T(8,128)(2,1)}, bf1...) custom-call(s32[2,2,4,128]{3,2,1,0:T(4,128)} %pad_add_fusion.refs_10, ...), custom_call_target="tpu_custom_call" | custom-call | flops 3623878656 | bytes 15728640 | tf_op jit(solution)/shard_map/feed_second/pallas_call | solution.py:292
  242.2 2.4 add_convert_fusion.2
  250.2 2.9 collective-permute-done.49.refs_2_
  257.0 3.3 %collective-permute-done.52 = bf16[64,2048]{1,0:T(8,128)(2,1)S(1)} collective-permute-done((bf16[64,2048]{1,0:T(8,128)(2,1)}, bf16[64,2048]{1,0:T(8,128)(2,1)S(1)}, u32[]{:S(2)}, u32[]{:S(2)}) %collective-permute-start.52) | collective-permute-done | bytes 262176 | tf_op jit(solution)/shard_map/ppermute | solution.py:28
  261.5 8.3 %collective-permute-done.54 = bf16[64,2048]{1,0:T(8,128)(2,1)S(1)} collective-permute-done((bf16[64,2048]{1,0:T(8,128)(2,1)}, bf16[64,2048]{1,0:T(8,128)(2,1)S(1)}, u32[]{:S(2)}, u32[]{:S(2)}) %collective-permute-start.54) | collective-permute-done | bytes 262176 | tf_op jit(solution)/shard_map/ppermute | solution.py:24
  275.3 3.6 %collective-permute-done.53 = bf16[128,2048]{1,0:T(8,128)(2,1)S(1)} collective-permute-done((bf16[128,2048]{1,0:T(8,128)(2,1)S(1)}, bf16[128,2048]{1,0:T(8,128)(2,1)S(1)}, u32[]{:S(2)}, u32[]{:S(2)}) %collective-permute-start.53) | collective-permute-done | bytes 524320 | tf_op jit(solution)/shard_map/ppermute | solution.py:24
  280.2 3.0 %collective-permute-done.51 = bf16[128,2048]{1,0:T(8,128)(2,1)S(1)} collective-permute-done((bf16[128,2048]{1,0:T(8,128)(2,1)S(1)}, bf16[128,2048]{1,0:T(8,128)(2,1)S(1)}, u32[]{:S(2)}, u32[]{:S(2)}) %collective-permute-start.51) | collective-permute-done | bytes 524320 | tf_op jit(solution)/shard_map/ppermute | solution.py:37
  283.2 2.4 fusion.2
  (253 shorter events, 105.3 us)
Async XLA Ops:
  0.0 51.7 %collective-permute-start.13 = (bf16[2048,768]{1,0:T(8,128)(2,1)}, bf16[2048,768]{1,0:T(8,128)(2,1)S(1)}, u32[]{:S(2)}, u32[]{:S(2)}) collective-permute-start(bf16[2048,768]{1,0:T(8,128)(2,1)} %bitcast.42), channel_id=1, source_target_pairs={{0,1},{1,0},{2,3},{3,2},{4,5},{5,4},{6,7},{7,6},{8,9},{9,8},{10,11... | collective-permute-start | bytes 9437192 | tf_op jit(solution)/shard_map/ppermute | solution.py:32
  0.5 53.8 %collective-permute-start.14 = (bf16[2048,768]{1,0:T(8,128)(2,1)}, bf16[2048,768]{1,0:T(8,128)(2,1)}, u32[]{:S(2)}, u32[]{:S(2)}) collective-permute-start(bf16[2048,768]{1,0:T(8,128)(2,1)} %bitcast.45), channel_id=1, source_target_pairs={{0,1},{1,0},{2,3},{3,2},{4,5},{5,4},{6,7},{7,6},{8,9},{9,8},{10,11... | collective-permute-start | bytes 9437192 | tf_op jit(solution)/shard_map/ppermute | solution.py:32
  0.5 55.2 %collective-permute-start.15 = (bf16[768,2048]{1,0:T(8,128)(2,1)}, bf16[768,2048]{1,0:T(8,128)(2,1)}, u32[]{:S(2)}, u32[]{:S(2)}) collective-permute-start(bf16[768,2048]{1,0:T(8,128)(2,1)} %bitcast.48), channel_id=1, source_target_pairs={{0,1},{1,0},{2,3},{3,2},{4,5},{5,4},{6,7},{7,6},{8,9},{9,8},{10,11... | collective-permute-start | bytes 9437192 | tf_op jit(solution)/shard_map/ppermute | solution.py:32
  4.2 14.8 %collective-permute-start.1 = (bf16[512,256]{1,0:T(8,128)(2,1)}, bf16[512,256]{1,0:T(8,128)(2,1)}, u32[]{:S(2)}, u32[]{:S(2)}) collective-permute-start(bf16[512,256]{1,0:T(8,128)(2,1)} %constant_dynamic-update-slice_fusion.refs_1_.refs_7_), channel_id=1, source_target_pairs={{0,4},{1,5},{2,6},{3,7},{8,12},{9,13},{10,14},{11,15},{16,20},{17,... | collective-permute-start | bytes 786440 | tf_op jit(solution)/shard_map/ppermute | solution.py:43
  39.4 34.5 %collective-permute-start.8 = (f32[4,32,128]{2,1,0:T(8,128)S(1)}, f32[4,32,128]{2,1,0:T(8,128)}, u32[]{:S(2)}, u32[]{:S(2)}) collective-permute-start(f32[4,32,128]{2,1,0:T(8,128)S(1)} %get-tuple-element.102.refs_10_), channel_id=1, source_target_pairs={{0,6},{1,7},{2,0},{3,1},{4,2},{5,3},{6,4},{7,5},{8,14},{9,15},{10,... | collective-permute-start | bytes 196616 | tf_op jit(solution)/shard_map/ppermute | solution.py:37
  43.5 30.4 %collective-permute-start.9 = (f32[4,32,128]{2,1,0:T(8,128)S(1)}, f32[4,32,128]{2,1,0:T(8,128)}, u32[]{:S(2)}, u32[]{:S(2)}) collective-permute-start(f32[4,32,128]{2,1,0:T(8,128)S(1)} %get-tuple-element.102.refs_10_), channel_id=1, source_target_pairs={{0,4},{1,5},{2,6},{3,7},{4,0},{5,1},{6,2},{7,3},{8,12},{9,13},{10,... | collective-permute-start | bytes 196616 | tf_op jit(solution)/shard_map/ppermute | solution.py:37
  51.7 22.2 %collective-permute-start.10 = (f32[4,32,128]{2,1,0:T(8,128)S(1)}, f32[4,32,128]{2,1,0:T(8,128)}, u32[]{:S(2)}, u32[]{:S(2)}) collective-permute-start(f32[4,32,128]{2,1,0:T(8,128)S(1)} %get-tuple-element.102.refs_10_), channel_id=1, source_target_pairs={{0,2},{1,3},{2,4},{3,5},{4,6},{5,7},{6,0},{7,1},{8,10},{9,11},{10,... | collective-permute-start | bytes 196616 | tf_op jit(solution)/shard_map/ppermute | solution.py:37
  54.3 17.9 %collective-permute-start.11 = (bf16[64,2048]{1,0:T(8,128)(2,1)}, bf16[64,2048]{1,0:T(8,128)(2,1)S(1)}, u32[]{:S(2)}, u32[]{:S(2)}) collective-permute-start(bf16[64,2048]{1,0:T(8,128)(2,1)} %get-tuple-element.98), channel_id=1, source_target_pairs={{0,8},{8,0},{16,24},{24,16},{1,9},{9,1},{17,25},{25,17},{2,10},{10... | collective-permute-start | bytes 786440 | tf_op jit(solution)/shard_map/ppermute | solution.py:24
  65.5 15.0 %collective-permute-start.16 = (bf16[128,2048]{1,0:T(8,128)(2,1)S(1)}, bf16[128,2048]{1,0:T(8,128)(2,1)S(1)}, u32[]{:S(2)}, u32[]{:S(2)}) collective-permute-start(bf16[128,2048]{1,0:T(8,128)(2,1)S(1)} %pad_maximum_fusion), channel_id=1, source_target_pairs={{0,8},{8,0},{16,24},{24,16},{1,9},{9,1},{17,25},{25,17},{2,10},{10... | collective-permute-start | bytes 1572872 | tf_op jit(solution)/shard_map/ppermute | solution.py:24
  72.3 14.5 %collective-permute-start.17 = (bf16[128,2048]{1,0:T(8,128)(2,1)S(1)}, bf16[128,2048]{1,0:T(8,128)(2,1)S(1)}, u32[]{:S(2)}, u32[]{:S(2)}) collective-permute-start(bf16[128,2048]{1,0:T(8,128)(2,1)S(1)} %pad_maximum_fusion.1), channel_id=1, source_target_pairs={{0,16},{8,24},{16,0},{24,8},{1,17},{9,25},{17,1},{25,9},{2,18},{10... | collective-permute-start | bytes 1572872 | tf_op jit(solution)/shard_map/ppermute | solution.py:28
  91.4 19.6 %collective-permute-start.18 = (bf16[128,2048]{1,0:T(8,128)(2,1)S(1)}, bf16[128,2048]{1,0:T(8,128)(2,1)}, u32[]{:S(2)}, u32[]{:S(2)}) collective-permute-start(bf16[128,2048]{1,0:T(8,128)(2,1)S(1)} %multiply_convert_fusion.refs_5_), channel_id=1, source_target_pairs={{0,6},{1,7},{2,0},{3,1},{4,2},{5,3},{6,4},{7,5},{8,14},{9,15},{10,... | collective-permute-start | bytes 1572872 | tf_op jit(solution)/shard_map/ppermute | solution.py:37
  104.6 29.2 %collective-permute-start.25 = (bf16[128,2048]{1,0:T(8,128)(2,1)}, bf16[128,2048]{1,0:T(8,128)(2,1)S(1)}, u32[]{:S(2)}, u32[]{:S(2)}) collective-permute-start(bf16[128,2048]{1,0:T(8,128)(2,1)} %hold.14), channel_id=1, source_target_pairs={{0,4},{1,5},{2,6},{3,7},{4,0},{5,1},{6,2},{7,3},{8,12},{9,13},{10,... | collective-permute-start | bytes 1572872 | tf_op jit(solution)/shard_map/ppermute | solution.py:37
  111.0 22.8 %collective-permute-start.21 = (bf16[128,2048]{1,0:T(8,128)(2,1)}, bf16[128,2048]{1,0:T(8,128)(2,1)S(1)}, u32[]{:S(2)}, u32[]{:S(2)}) collective-permute-start(bf16[128,2048]{1,0:T(8,128)(2,1)} %hold.13.refs_0_), channel_id=1, source_target_pairs={{0,8},{8,0},{16,24},{24,16},{1,9},{9,1},{17,25},{25,17},{2,10},{10... | collective-permute-start | bytes 1572872 | tf_op jit(solution)/shard_map/ppermute | solution.py:24
  112.1 21.6 %collective-permute-start.22 = (bf16[128,2048]{1,0:T(8,128)(2,1)}, bf16[128,2048]{1,0:T(8,128)(2,1)S(1)}, u32[]{:S(2)}, u32[]{:S(2)}) collective-permute-start(bf16[128,2048]{1,0:T(8,128)(2,1)} %hold.13.refs_0_), channel_id=1, source_target_pairs={{0,16},{8,24},{16,0},{24,8},{1,17},{9,25},{17,1},{25,9},{2,18},{10... | collective-permute-start | bytes 1572872 | tf_op jit(solution)/shard_map/ppermute | solution.py:28
  112.4 17.0 %collective-permute-start.26 = (bf16[64,2048]{1,0:T(8,128)(2,1)}, bf16[64,2048]{1,0:T(8,128)(2,1)S(1)}, u32[]{:S(2)}, u32[]{:S(2)}) collective-permute-start(bf16[64,2048]{1,0:T(8,128)(2,1)} %slice.158.refs_1_), channel_id=1, source_target_pairs={{0,16},{8,24},{16,0},{24,8},{1,17},{9,25},{17,1},{25,9},{2,18},{10... | collective-permute-start | bytes 786440 | tf_op jit(solution)/shard_map/ppermute | solution.py:28
  114.2 15.3 %collective-permute-start.27 = (bf16[64,2048]{1,0:T(8,128)(2,1)}, bf16[64,2048]{1,0:T(8,128)(2,1)S(1)}, u32[]{:S(2)}, u32[]{:S(2)}) collective-permute-start(bf16[64,2048]{1,0:T(8,128)(2,1)} %slice.159.refs_2_), channel_id=1, source_target_pairs={{0,8},{8,0},{16,24},{24,16},{1,9},{9,1},{17,25},{25,17},{2,10},{10... | collective-permute-start | bytes 786440 | tf_op jit(solution)/shard_map/ppermute | solution.py:24
  135.6 15.1 %collective-permute-start.28 = (bf16[128,2048]{1,0:T(8,128)(2,1)}, bf16[128,2048]{1,0:T(8,128)(2,1)S(1)}, u32[]{:S(2)}, u32[]{:S(2)}) collective-permute-start(bf16[128,2048]{1,0:T(8,128)(2,1)} %hold.15.refs_5_), channel_id=1, source_target_pairs={{0,8},{8,0},{16,24},{24,16},{1,9},{9,1},{17,25},{25,17},{2,10},{10... | collective-permute-start | bytes 1572872 | tf_op jit(solution)/shard_map/ppermute | solution.py:24
  136.2 16.8 %collective-permute-start.29 = (bf16[128,2048]{1,0:T(8,128)(2,1)}, bf16[128,2048]{1,0:T(8,128)(2,1)S(1)}, u32[]{:S(2)}, u32[]{:S(2)}) collective-permute-start(bf16[128,2048]{1,0:T(8,128)(2,1)} %hold.15.refs_5_), channel_id=1, source_target_pairs={{0,16},{8,24},{16,0},{24,8},{1,17},{9,25},{17,1},{25,9},{2,18},{10... | collective-permute-start | bytes 1572872 | tf_op jit(solution)/shard_map/ppermute | solution.py:28
  141.6 15.1 %collective-permute-start.32 = (bf16[128,2048]{1,0:T(8,128)(2,1)}, bf16[128,2048]{1,0:T(8,128)(2,1)}, u32[]{:S(2)}, u32[]{:S(2)}) collective-permute-start(bf16[128,2048]{1,0:T(8,128)(2,1)} %hold.16), channel_id=1, source_target_pairs={{0,2},{1,3},{2,4},{3,5},{4,6},{5,7},{6,0},{7,1},{8,10},{9,11},{10,... | collective-permute-start | bytes 1572872 | tf_op jit(solution)/shard_map/ppermute | solution.py:37
  141.6 15.1 %collective-permute-start.23 = (bf16[64,2048]{1,0:T(8,128)(2,1)}, bf16[64,2048]{1,0:T(8,128)(2,1)S(1)}, u32[]{:S(2)}, u32[]{:S(2)}) collective-permute-start(bf16[64,2048]{1,0:T(8,128)(2,1)} %slice.156.refs_1_), channel_id=1, source_target_pairs={{0,16},{8,24},{16,0},{24,8},{1,17},{9,25},{17,1},{25,9},{2,18},{10... | collective-permute-start | bytes 786440 | tf_op jit(solution)/shard_map/ppermute | solution.py:28
  142.6 14.1 %collective-permute-start.24 = (bf16[64,2048]{1,0:T(8,128)(2,1)}, bf16[64,2048]{1,0:T(8,128)(2,1)S(1)}, u32[]{:S(2)}, u32[]{:S(2)}) collective-permute-start(bf16[64,2048]{1,0:T(8,128)(2,1)} %slice.157.refs_2_), channel_id=1, source_target_pairs={{0,8},{8,0},{16,24},{24,16},{1,9},{9,1},{17,25},{25,17},{2,10},{10... | collective-permute-start | bytes 786440 | tf_op jit(solution)/shard_map/ppermute | solution.py:24
  157.5 17.6 %collective-permute-start.33 = (bf16[128,2048]{1,0:T(8,128)(2,1)}, bf16[128,2048]{1,0:T(8,128)(2,1)S(1)}, u32[]{:S(2)}, u32[]{:S(2)}) collective-permute-start(bf16[128,2048]{1,0:T(8,128)(2,1)} %hold.17.refs_0_), channel_id=1, source_target_pairs={{0,8},{8,0},{16,24},{24,16},{1,9},{9,1},{17,25},{25,17},{2,10},{10... | collective-permute-start | bytes 1572872 | tf_op jit(solution)/shard_map/ppermute | solution.py:24
  159.1 16.0 %collective-permute-start.34 = (bf16[128,2048]{1,0:T(8,128)(2,1)}, bf16[128,2048]{1,0:T(8,128)(2,1)S(1)}, u32[]{:S(2)}, u32[]{:S(2)}) collective-permute-start(bf16[128,2048]{1,0:T(8,128)(2,1)} %hold.17.refs_0_), channel_id=1, source_target_pairs={{0,16},{8,24},{16,0},{24,8},{1,17},{9,25},{17,1},{25,9},{2,18},{10... | collective-permute-start | bytes 1572872 | tf_op jit(solution)/shard_map/ppermute | solution.py:28
  177.1 15.4 %collective-permute-start.35 = (bf16[64,2048]{1,0:T(8,128)(2,1)S(1)}, bf16[64,2048]{1,0:T(8,128)(2,1)S(1)}, u32[]{:S(2)}, u32[]{:S(2)}) collective-permute-start(bf16[64,2048]{1,0:T(8,128)(2,1)S(1)} %slice.130), channel_id=1, source_target_pairs={{0,16},{8,24},{16,0},{24,8},{1,17},{9,25},{17,1},{25,9},{2,18},{10... | collective-permute-start | bytes 786440 | tf_op jit(solution)/shard_map/ppermute | solution.py:28
  201.8 23.7 %collective-permute-start.40 = (bf16[128,2048]{1,0:T(8,128)(2,1)}, bf16[128,2048]{1,0:T(8,128)(2,1)S(1)}, u32[]{:S(2)}, u32[]{:S(2)}) collective-permute-start(bf16[128,2048]{1,0:T(8,128)(2,1)} %pad_maximum_fusion.3), channel_id=1, source_target_pairs={{0,16},{8,24},{16,0},{24,8},{1,17},{9,25},{17,1},{25,9},{2,18},{10... | collective-permute-start | bytes 1572872 | tf_op jit(solution)/shard_map/ppermute | solution.py:28
  206.2 19.4 %collective-permute-start.38 = (bf16[128,2048]{1,0:T(8,128)(2,1)}, bf16[128,2048]{1,0:T(8,128)(2,1)S(1)}, u32[]{:S(2)}, u32[]{:S(2)}) collective-permute-start(bf16[128,2048]{1,0:T(8,128)(2,1)} %pad_maximum_fusion.2), channel_id=1, source_target_pairs={{0,8},{8,0},{16,24},{24,16},{1,9},{9,1},{17,25},{25,17},{2,10},{10... | collective-permute-start | bytes 1572872 | tf_op jit(solution)/shard_map/ppermute | solution.py:24
  223.0 17.3 %collective-permute-start.45 = (bf16[128,2048]{1,0:T(8,128)(2,1)S(1)}, bf16[128,2048]{1,0:T(8,128)(2,1)S(1)}, u32[]{:S(2)}, u32[]{:S(2)}) collective-permute-start(bf16[128,2048]{1,0:T(8,128)(2,1)S(1)} %pad_maximum_fusion.5), channel_id=1, source_target_pairs={{0,16},{8,24},{16,0},{24,8},{1,17},{9,25},{17,1},{25,9},{2,18},{10... | collective-permute-start | bytes 1572872 | tf_op jit(solution)/shard_map/ppermute | solution.py:28
  223.7 16.6 %collective-permute-start.43 = (bf16[128,2048]{1,0:T(8,128)(2,1)S(1)}, bf16[128,2048]{1,0:T(8,128)(2,1)S(1)}, u32[]{:S(2)}, u32[]{:S(2)}) collective-permute-start(bf16[128,2048]{1,0:T(8,128)(2,1)S(1)} %pad_maximum_fusion.4), channel_id=1, source_target_pairs={{0,8},{8,0},{16,24},{24,16},{1,9},{9,1},{17,25},{25,17},{2,10},{10... | collective-permute-start | bytes 1572872 | tf_op jit(solution)/shard_map/ppermute | solution.py:24
  228.0 47.3 %collective-permute-start.41 = (bf16[128,2048]{1,0:T(8,128)(2,1)}, bf16[128,2048]{1,0:T(8,128)(2,1)}, u32[]{:S(2)}, u32[]{:S(2)}) collective-permute-start(bf16[128,2048]{1,0:T(8,128)(2,1)} %add_convert_fusion.3), channel_id=1, source_target_pairs={{0,4},{1,5},{2,6},{3,7},{4,0},{5,1},{6,2},{7,3},{8,12},{9,13},{10,... | collective-permute-start | bytes 1572872 | tf_op jit(solution)/shard_map/ppermute | solution.py:37
  244.7 30.7 %collective-permute-start.46 = (bf16[128,2048]{1,0:T(8,128)(2,1)}, bf16[128,2048]{1,0:T(8,128)(2,1)S(1)}, u32[]{:S(2)}, u32[]{:S(2)}) collective-permute-start(bf16[128,2048]{1,0:T(8,128)(2,1)} %add_convert_fusion.2), channel_id=1, source_target_pairs={{0,2},{1,3},{2,4},{3,5},{4,6},{5,7},{6,0},{7,1},{8,10},{9,11},{10,... | collective-permute-start | bytes 1572872 | tf_op jit(solution)/shard_map/ppermute | solution.py:37
  249.9 21.0 %collective-permute-start.48 = (bf16[128,2048]{1,0:T(8,128)(2,1)}, bf16[128,2048]{1,0:T(8,128)(2,1)}, u32[]{:S(2)}, u32[]{:S(2)}) collective-permute-start(bf16[128,2048]{1,0:T(8,128)(2,1)} %pad_maximum_fusion.6), channel_id=1, source_target_pairs={{0,8},{8,0},{16,24},{24,16},{1,9},{9,1},{17,25},{25,17},{2,10},{10... | collective-permute-start | bytes 1572872 | tf_op jit(solution)/shard_map/ppermute | solution.py:24
  256.6 16.1 %collective-permute-start.50 = (bf16[128,2048]{1,0:T(8,128)(2,1)S(1)}, bf16[128,2048]{1,0:T(8,128)(2,1)S(1)}, u32[]{:S(2)}, u32[]{:S(2)}) collective-permute-start(bf16[128,2048]{1,0:T(8,128)(2,1)S(1)} %pad_maximum_fusion.7), channel_id=1, source_target_pairs={{0,16},{8,24},{16,0},{24,8},{1,17},{9,25},{17,1},{25,9},{2,18},{10... | collective-permute-start | bytes 1572872 | tf_op jit(solution)/shard_map/ppermute | solution.py:28
  (66 other events, 569.5 us)
